TPU v7x, 512 devices: a whole 4x4x16 slice. The times are simulated.
512 devices in a mesh: rep: 16 (over z_hi, y), fsdp: 32 (over z_lo, x, core).
Axes of the slice: x: 4, y: 4, z: 16 (z_hi: 4, z_lo: 4; z = z_hi * 4 + z_lo), core: 2. Of those that a mesh axis runs over, the one named last changes fastest.
Arguments:
- activations: bfloat16 [65536, 5120], P(('rep', 'fsdp')), may hold values from -6 to 6
- out_grad: bfloat16 [65536, 128], P(('rep', 'fsdp')), may hold values from -0.09375 to 0.09375
- momentum: float32 [16, 160, 64, 64], P('rep', 'fsdp'), may hold values from -6 to 6
- weight: float32 [160, 64, 64], P('fsdp'), may hold values from -6 to 6
- kept_tile: int32 [16, 160], P('rep', 'fsdp'), may hold values from 0 to 63
Outputs:
- new_momentum: float32 [16, 160, 64, 64], P('rep', 'fsdp')
- new_weight: float32 [160, 64, 64], P('fsdp')
Inputs may be any that keep to these rules, and one draw needn't show every extreme that they name: `kept_tile`: tile number t names the tile in block row t // 8 and block column t % (8) of a span's coefficients.
All inputs are finite; a program needn't handle non-finite values.
Results may differ from a plain program's by a relative error of at most 0.0003.
Values sent between devices are 32-bit elements; how exact they have to be, the bound alone decides.
A program may use at most 64 MiB of HBM per device.

v0:
```python
import math

import jax
import jax.numpy as jnp
from jax import lax
from jax.sharding import PartitionSpec as P

SPAN = 64
TILE = 8


decay_rate = 0.9
step_size = 0.5
epsilon = 1e-06


def dct_basis():
    freq = jnp.arange(SPAN, dtype=jnp.float32)[:, None]
    place = jnp.arange(SPAN, dtype=jnp.float32)[None, :]
    factor = jnp.where(freq == 0, math.sqrt(1.0 / SPAN), math.sqrt(2.0 / SPAN))
    return factor * jnp.cos(math.pi * (2.0 * place + 1.0) * freq / (2.0 * SPAN))


def selectors(index, blocks):
    per_side = SPAN // TILE
    levels = jnp.arange(per_side, dtype=jnp.int32)
    hot_a = ((index // per_side)[..., None] == levels).astype(jnp.float32)
    hot_b = ((index % per_side)[..., None] == levels).astype(jnp.float32)
    rows_a = jnp.einsum("gka,apu->gkpu", hot_a, blocks, precision=lax.Precision.HIGHEST)
    rows_b = jnp.einsum("gka,apu->gkpu", hot_b, blocks, precision=lax.Precision.HIGHEST)
    return (rows_a, rows_b)


def shards(activations, out_grad, momentum, weight, kept_tile):
    col_blocks = activations.shape[1] // SPAN
    row_blocks = out_grad.shape[1] // SPAN
    product = jnp.einsum("tr,td->rd", out_grad, activations, preferred_element_type=jnp.float32)
    pieces = product.reshape(row_blocks, SPAN, col_blocks, SPAN)
    pieces = pieces.transpose(0, 2, 1, 3).reshape(row_blocks * col_blocks, SPAN, SPAN)
    owned = lax.psum_scatter(pieces, "fsdp", scatter_dimension=0, tiled=True)
    state = decay_rate * momentum + owned[None]
    basis = dct_basis()
    blocks = basis.reshape(SPAN // TILE, TILE, SPAN)
    rows_a, rows_b = selectors(kept_tile, blocks)
    tiles = jnp.einsum(
        "gkpi,gkij,gkqj->gkpq", rows_a, state, rows_b, precision=lax.Precision.HIGHEST
    )
    decoded = jnp.einsum(
        "gkpi,gkpq,gkqj->gkij", rows_a, tiles, rows_b, precision=lax.Precision.HIGHEST
    )
    new_momentum = state - decoded
    every_tile, every_number = (
        lax.all_gather(tiles, "rep", axis=0, tiled=True),
        lax.all_gather(kept_tile.astype(jnp.float32), "rep", axis=0, tiled=True),
    )
    every_index = every_number.astype(jnp.int32)
    other_a, other_b = selectors(every_index, blocks)
    update = jnp.einsum(
        "gkpi,gkpq,gkqj->kij", other_a, every_tile, other_b, precision=lax.Precision.HIGHEST
    )
    spread = jnp.sqrt(jnp.mean(update * update, axis=(1, 2), keepdims=True) + epsilon)
    new_weight = weight - step_size * update / spread
    return (new_momentum, new_weight)


def solution(mesh):
    placed = (
        P(("rep", "fsdp"), None),
        P(("rep", "fsdp"), None),
        P("rep", "fsdp", None, None),
        P("fsdp", None, None),
        P("rep", "fsdp"),
    )
    return jax.shard_map(
        shards,
        mesh=mesh,
        in_specs=placed,
        out_specs=(P("rep", "fsdp", None, None), P("fsdp", None, None)),
        check_vma=False,
    )
```

profile of v0, /device:TPU:1, one launch (start us, length us, event | category | flops | bytes accessed | tf_op | source)
XLA Modules:
  0.0 241.8 jit_solution(1953620292594766515)
XLA Ops:
  7.2 0.0 copy-start
  7.2 0.0 reduce-scatter.2.cloned.1.call-start
  7.2 1.3 copy-done
  8.5 2.8 %fusion.56 = f32[128,5120]{1,0:T(8,128)} fusion(bf16[128,128]{1,0:T(8,128)(2,1)} %param.6, bf16[128,5120]{1,0:T(8,128)(2,1)S(1)} %copy-done), kind=kOutput, calls=%fused_computation.79 | convolution fusion | flops 167772160 | bytes 3964928 | tf_op jit(solution)/shard_map/tr,td->rd/dot_general | solution.py:37
  11.3 5.1 %reshape.152 = f32[2,64,80,64]{3,2,1,0:T(8,128)} reshape(f32[128,5120]{1,0:T(8,128)} %fusion.56) | data formatting | bytes 5242880 | tf_op jit(solution)/shard_map/reshape | solution.py:38
  16.4 6.4 %copy.19 = f32[2,80,64,64]{3,2,1,0:T(8,128)} copy(f32[2,80,64,64]{3,1,2,0:T(8,128)} %bitcast.81) | data formatting | bytes 5242880 | tf_op jit(solution)/shard_map/transpose | solution.py:39
  22.7 0.0 copy-start.4
  22.7 0.0 copy-start.1
  22.7 0.0 reduce-scatter.2.cloned.1.call-update
  22.8 0.6 copy-done.4
  23.4 0.0 copy-start.3
  23.4 51.9 %all-gather.1 = f32[16,1,5]{2,1,0:T(1,128)S(1)} all-gather(f32[1,1,5]{2,1,0:T(1,128)S(1)} %get-tuple-element.4), channel_id=1, replica_groups=mesh['rep'=16,'fsdp'=32] {'rep'}, dimensions={0}, use_global_device_ids=true | all-gather | bytes 340 | tf_op jit(solution)/shard_map/all_gather | solution.py:54
  75.3 0.1 copy.26
  75.5 0.3 fusion.11
  75.8 0.3 fusion.10
  76.1 0.5 fusion.8
  76.6 0.5 fusion.6
  77.1 104.3 %reduce-scatter.2.cloned.1.call-done = f32[5,64,64]{2,1,0:T(8,128)} async-done(((f32[160,64,64]{2,1,0:T(8,128)}), f32[5,64,64]{2,1,0:T(8,128)}) %reduce-scatter.2.cloned.1.call-update) | async-done | bytes 81936 | tf_op jit(solution)/shard_map/reduce_scatter | solution.py:40
  181.4 0.0 copy-done.1
  181.4 0.0 copy-start.2
  181.4 1.2 fusion.4
  182.6 0.2 fusion.33
  182.8 0.2 fusion.35
  183.0 48.3 %all-gather = f32[80,8,8]{2,1,0:T(8,128)S(1)} all-gather(f32[5,8,8]{2,1,0:T(8,128)S(1)} %fusion.33), channel_id=2, replica_groups=mesh['rep'=16,'fsdp'=32] {'rep'}, dimensions={0}, use_global_device_ids=true | all-gather | bytes 21760 | tf_op jit(solution)/shard_map/all_gather | solution.py:53
  231.4 0.9 fusion.2
  232.2 0.8 multiply_reduce_fusion
  233.1 0.0 copy-done.3
  233.1 0.8 divide_subtract_fusion
  233.8 0.0 copy-done.2
  233.8 1.1 fusion
  (5 shorter events, 0.1 us)
Async XLA Ops:
  7.2 1.3 copy-start
  7.2 174.2 %reduce-scatter.2.cloned.1.call-start = ((), (), s32[]{:S(2)}) async-start(), calls=%async_computation.1 | async-start | bytes 5406720 | tf_op jit(solution)/shard_map/reduce_scatter | solution.py:40
  22.7 0.7 copy-start.4
  22.7 158.6 %copy-start.1 = (f32[1,5,64,64]{3,2,1,0:T(8,128)S(1)}, f32[1,5,64,64]{3,2,1,0:T(8,128)}, u32[]{:S(2)}) copy-start(f32[1,5,64,64]{3,2,1,0:T(8,128)} %param.7) | copy-start | bytes 245764
  23.4 209.7 %copy-start.3 = (f32[5,64,64]{2,1,0:T(8,128)S(1)}, f32[5,64,64]{2,1,0:T(8,128)}, u32[]{:S(2)}) copy-start(f32[5,64,64]{2,1,0:T(8,128)} %param.8) | copy-start | bytes 245764
  181.4 52.5 %copy-start.2 = (f32[5,64,64]{2,1,0:T(8,128)S(1)}, f32[5,64,64]{2,1,0:T(8,128)}, u32[]{:S(2)}) copy-start(f32[5,64,64]{2,1,0:T(8,128)} %reduce-scatter.2.cloned.1.call-done) | copy-start | bytes 245764
Sparse Core Ops, SparseCore 0:
  22.9 158.4 reduce-scatter.1
where the time goes:
time: 246 us; the launch traced here: 242 us
  waiting for transfers between devices  104 us (42%)
  blocking collectives  100 us (41%)
  between operations  14.1 us (6%)
  local copies, waits for them, and re-layouts  13.5 us (5%)
  matrix products  8.78 us (4%)
    reduce_scatter x1, waiting for transfers between devices, shards(): owned = lax.psum_scatter(pieces, 'fsdp', scatter_dimension=0, tiled=True)  104 us
    all_gather x1, blocking collectives, shards(): lax.all_gather(kept_tile.astype(jnp.float32), 'rep', axis=0, tiled=True)  51.9 us
    all_gather x1, blocking collectives, shards(): lax.all_gather(tiles, 'rep', axis=0, tiled=True)  48.3 us
    transpose x1, local copies, waits for them, and re-layouts, shards(): pieces.transpose(0, 2, 1, 3).reshape(row_blocks * col_blocks, SPAN, SPAN)  6.37 us
    reshape x1, local copies, waits for them, and re-layouts, shards(): pieces = product.reshape(row_blocks, SPAN, col_blocks, SPAN)  5.09 us
  transfers between devices with their start and end apart: 1, of which 1 were waited for; matrix products, arithmetic and copies ran while one was open for 1% of the time, Pallas kernels for 0%

commit v1 on v0

v1 whole, which is shorter than its diff:
```python
import functools

import jax
import jax.numpy as jnp
import numpy as np
from jax import lax
from jax.experimental import pallas as pl
from jax.experimental.pallas import tpu as pltpu
from jax.sharding import PartitionSpec as P

SPAN = 64
TILE = 8
N_X = 4
N_ZLO = 4
N_REP = 16
SLAB = 160
HALF = SLAB // 2
TOK = 128
COLS = 5120
WIDE = 640
PARITY = 4 * WIDE

decay_rate = 0.9
step_size = 0.5
epsilon = 1e-06

MESH = pl.DeviceIdType.MESH
HI = lax.Precision.HIGHEST


def tables():
    u = np.arange(SPAN, dtype=np.float64)[:, None]
    x = np.arange(SPAN, dtype=np.float64)[None, :]
    s = np.where(u == 0, np.sqrt(1.0 / SPAN), np.sqrt(2.0 / SPAN))
    basis = s * np.cos(np.pi * (2.0 * x + 1.0) * u / (2.0 * SPAN))
    zero = np.zeros((SPAN, SPAN))
    rows = [
        np.concatenate([basis, zero], 1),
        np.concatenate([basis.T, zero], 1),
        np.block([[basis.T, zero], [zero, basis.T]]),
        np.block([[basis, zero], [zero, basis]]),
    ]
    return np.concatenate(rows, 0).astype(np.float32)


def dot32(a, b):
    return jnp.dot(a, b, precision=HI, preferred_element_type=jnp.float32)


def left(table, parts):
    wide = dot32(table, jnp.concatenate(parts, axis=1))
    return [wide[:, 128 * p : 128 * p + 128] for p in range(3)]


def right(parts, table):
    tall = dot32(jnp.concatenate(parts, axis=0), table)
    return [tall[SPAN * p : SPAN * p + SPAN] for p in range(3)]


def kernel(
    acts_h, outg_h, mom_h, wt_h, kept_h, cst_h,
    newm_h, neww_h,
    acts, outg, mom, wt, kept, cst,
    part, rx, x1, x0, x2, zr, every, outm, outw,
    lsem, osem, csend, crecv, xsend, xrecv, zsend, zrecv, gsend, grecv,
):
    rep = lax.axis_index("rep")
    f = lax.axis_index("fsdp")
    core = lax.rem(f, 2)
    x = lax.rem(f // 2, N_X)
    z = f // (2 * N_X)
    other = 1 - core
    xr, xl, xo = lax.rem(x + 1, N_X), lax.rem(x + 3, N_X), lax.rem(x + 2, N_X)

    def at(z_, x_, core_):
        return (rep, (z_ * N_X + x_) * 2 + core_)

    piece = [lax.rem(z + d, N_ZLO) for d in (1, 3, 2)] + [z]

    first = lax.rem(z + 1, 2)
    load_acts = []
    for k in range(2):
        par = first if k == 0 else 1 - first
        cols = pl.ds(pl.multiple_of(par * PARITY, 128), PARITY)
        load_acts.append(pltpu.make_async_copy(acts_h.at[:, cols], acts.at[:, cols], lsem.at[k]))
    load_outg = pltpu.make_async_copy(outg_h, outg, lsem.at[2])
    load_outg.start()
    load_acts[0].start()
    load_acts[1].start()
    small = [
        pltpu.make_async_copy(src, dst, lsem.at[3 + i])
        for i, (src, dst) in enumerate(((mom_h.at[0], mom), (wt_h, wt), (kept_h, kept), (cst_h, cst)))
    ]
    for copy in small:
        copy.start()

    barrier = pltpu.get_barrier_semaphore()
    near = [at(z, x, other), at(z, xr, core), at(z, xl, core)] + [at(piece[k], x, core) for k in range(3)]
    for peer in near:
        pl.semaphore_signal(barrier, inc=1, device_id=peer, device_id_type=MESH)

    def greet(i, carry):
        pl.semaphore_signal(
            barrier, inc=1, device_id=(lax.rem(rep + i, N_REP), f), device_id_type=MESH
        )
        return carry

    lax.fori_loop(1, N_REP, greet, 0)

    lane = lax.broadcasted_iota(jnp.int32, (32, 128), 1)

    def product(par, grads):
        def chunk(j, carry):
            base = pl.multiple_of(par * PARITY + j * WIDE, 128)
            prod = jnp.dot(grads, acts[:, pl.ds(base, WIDE)], preferred_element_type=jnp.float32)
            for h in range(2):
                blk = prod[SPAN * h : SPAN * h + SPAN]
                zz = 2 * h + par
                b2 = blk[:, 256:384]
                part[0, zz, j, 0:64] = blk[:, 0:128]
                part[0, zz, j, 64:128] = blk[:, 128:256]
                part[0, zz, j, 128:160] = jnp.where(lane < 64, b2[0:32], pltpu.roll(b2[32:64], 64, 1))
                part[1, zz, j, 0:64] = blk[:, 384:512]
                part[1, zz, j, 64:128] = blk[:, 512:640]
                part[1, zz, j, 128:160] = jnp.where(lane < 64, pltpu.roll(b2[0:32], 64, 1), b2[32:64])
            return carry

        lax.fori_loop(0, 4, chunk, 0)

    def swap(k):
        return pltpu.make_async_remote_copy(
            src_ref=part.at[other, piece[k]], dst_ref=rx.at[k],
            send_sem=csend.at[k], recv_sem=crecv.at[k],
            device_id=at(z, x, other), device_id_type=MESH,
        )

    A, B = pl.ds(0, HALF), pl.ds(HALF, HALF)

    def hop(k, kind, way):
        side = xr if way == 0 else xl
        slab = xo if kind == 1 else side
        rows = (B if way == 0 else A) if kind == 0 else (A if way == 0 else B)
        land = (x0, x1, x2)[kind]
        i = (k * 3 + kind) * 2 + way
        return pltpu.make_async_remote_copy(
            src_ref=part.at[core, piece[k], slab, rows], dst_ref=land.at[k, way],
            send_sem=xsend.at[i], recv_sem=xrecv.at[i],
            device_id=at(z, side, core), device_id_type=MESH,
        )

    def zhop(k):
        return pltpu.make_async_remote_copy(
            src_ref=part.at[core, piece[k], x], dst_ref=zr.at[k],
            send_sem=zsend.at[k], recv_sem=zrecv.at[k],
            device_id=at(piece[k], x, core), device_id_type=MESH,
        )

    def open_piece(k):
        swap(k).wait_recv()

        def add(j, carry):
            part[core, piece[k], j] = part[core, piece[k], j] + rx[k, j]
            return carry

        lax.fori_loop(0, N_X, add, 0)
        for kind in (1, 0):
            for way in range(2):
                hop(k, kind, way).start()

    def pass_on(k):
        for way in range(2):
            hop(k, 1, way).wait_recv()
            side, rows = (xr, A) if way == 0 else (xl, B)
            part[core, piece[k], side, rows] = part[core, piece[k], side, rows] + x1[k, way]
            hop(k, 2, way).start()

    def close_piece(k):
        for way in range(2):
            hop(k, 0, way).wait_recv()
            hop(k, 2, way).wait_recv()
        part[core, piece[k], x, A] = part[core, piece[k], x, A] + (x0[k, 1] + x2[k, 0])
        part[core, piece[k], x, B] = part[core, piece[k], x, B] + (x0[k, 0] + x2[k, 1])
        if k < 3:
            zhop(k).start()

    load_outg.wait()
    grads = outg[...].astype(jnp.float32).T.astype(jnp.bfloat16)
    load_acts[0].wait()
    product(first, grads)
    pl.semaphore_wait(barrier, len(near) + N_REP - 1)
    swap(0).start()
    swap(1).start()
    load_acts[1].wait()
    product(1 - first, grads)
    swap(2).start()
    swap(3).start()
    open_piece(0)
    open_piece(1)
    pass_on(0)
    open_piece(2)
    pass_on(1)
    close_piece(0)
    open_piece(3)
    pass_on(2)
    close_piece(1)
    pass_on(3)
    close_piece(2)

    for copy in small:
        copy.wait()
    order = [core, core + 1, core + 2, core + 3, 4 * other]
    numbers = [kept[0, s] for s in order]
    wide = lax.broadcasted_iota(jnp.int32, (SPAN, 128), 1)
    row = lax.broadcasted_iota(jnp.int32, (SPAN, 128), 0)
    place = (row // TILE) * TILE + lax.rem(wide, SPAN) // TILE

    def pairs(ref):
        zero = jnp.zeros((SPAN, SPAN), jnp.float32)
        return [
            jnp.concatenate([ref[order[0]], ref[order[1]]], axis=1),
            jnp.concatenate([ref[order[2]], ref[order[3]]], axis=1),
            jnp.concatenate([ref[order[4]], zero], axis=1),
        ]

    def unpair(ref, parts):
        ref[order[0]] = parts[0][:, :SPAN]
        ref[order[1]] = parts[0][:, SPAN:]
        ref[order[2]] = parts[1][:, :SPAN]
        ref[order[3]] = parts[1][:, SPAN:]
        ref[order[4]] = parts[2][:, :SPAN]

    carried = [decay_rate * m for m in pairs(mom)]
    keep = [
        place == jnp.where(wide < SPAN, numbers[2 * p], numbers[min(2 * p + 1, 4)]) for p in range(3)
    ]
    fwd_l, inv_l = cst[0:64, 0:64], cst[64:128, 0:64]
    fwd_r, inv_r = cst[128:256], cst[256:384]

    close_piece(3)
    for k in range(3):
        zhop(k).wait_recv()
    total = part[core, z, x] + (zr[0] + zr[1] + zr[2])
    tail = jnp.concatenate([total[128:160], pltpu.roll(total[128:160], 64, 1)], axis=0)
    state = [
        carried[0] + total[0:64],
        carried[1] + total[64:128],
        carried[2] + jnp.where(wide < SPAN, tail, 0.0),
    ]
    coef = right(left(fwd_l, state), fwd_r)
    kept_coef = [jnp.where(keep[p], coef[p], 0.0) for p in range(3)]

    lane8 = lax.broadcasted_iota(jnp.int32, (TILE, 128), 1)
    message = jnp.zeros((TILE, 128), jnp.float32)
    for j in range(5):
        tile = jnp.sum(kept_coef[j // 2].reshape(8, TILE, 128), axis=0)
        tile = jnp.where((lane8 < SPAN) == (j % 2 == 0), tile, 0.0)
        for shift in (8, 16, 32, 64):
            tile = tile + pltpu.roll(tile, shift, 1)
        message = jnp.where(lane8 // TILE == j, tile, message)
        message = jnp.where(lane8 == 40 + j, numbers[j].astype(jnp.float32), message)
    every[rep] = message

    def post(i):
        return pltpu.make_async_remote_copy(
            src_ref=every.at[rep], dst_ref=every.at[rep],
            send_sem=gsend.at[i], recv_sem=grecv.at[i],
            device_id=(lax.rem(rep + i, N_REP), f), device_id_type=MESH,
        )

    def arrival(i):
        slot = lax.rem(rep + N_REP - i, N_REP)
        return pltpu.make_async_remote_copy(
            src_ref=every.at[rep], dst_ref=every.at[slot],
            send_sem=gsend.at[i], recv_sem=grecv.at[i],
            device_id=(lax.rem(rep + i, N_REP), f), device_id_type=MESH,
        )

    def send_one(i, carry):
        post(i).start()
        return carry

    lax.fori_loop(1, N_REP, send_one, 0)

    decoded = left(inv_l, right(kept_coef, inv_r))
    unpair(outm, [state[p] - decoded[p] for p in range(3)])
    store_m = pltpu.make_async_copy(outm, newm_h.at[0], osem.at[0])
    store_m.start()
    weights = pairs(wt)

    def wait_one(i, carry):
        arrival(i).wait_recv()
        return carry

    lax.fori_loop(1, N_REP, wait_one, 0)

    src_tile = [8 * jnp.where(lane8 < SPAN, 2 * p, min(2 * p + 1, 4)) + lax.rem(lane8, 8) for p in range(3)]
    src_num = [40 + jnp.where(lane8 < SPAN, 2 * p, min(2 * p + 1, 4)) for p in range(3)]
    place_f = place.astype(jnp.float32).reshape(8, TILE, 128)

    def gather_one(g, sums):
        got = every[g]
        new = []
        for p in range(3):
            tile = jnp.take_along_axis(got, src_tile[p], axis=1)
            num = jnp.take_along_axis(got, src_num[p], axis=1)
            new.append(sums[p] + jnp.where(num[None] == place_f, tile[None], 0.0))
        return tuple(new)

    sums = lax.fori_loop(
        0, N_REP, gather_one, tuple(jnp.zeros((8, TILE, 128), jnp.float32) for _ in range(3))
    )
    update = left(inv_l, right([s.reshape(SPAN, 128) for s in sums], inv_r))
    fresh = []
    for p in range(3):
        square = jnp.sum(update[p] * update[p], axis=0, keepdims=True)
        low = wide[0:1] < SPAN
        mean_lo = jnp.sum(jnp.where(low, square, 0.0), axis=1, keepdims=True) / (SPAN * SPAN)
        mean_hi = jnp.sum(jnp.where(low, 0.0, square), axis=1, keepdims=True) / (SPAN * SPAN)
        spread = jnp.sqrt(jnp.where(low, mean_lo, mean_hi) + epsilon)
        fresh.append(weights[p] - step_size * update[p] / spread)
    unpair(outw, fresh)
    store_w = pltpu.make_async_copy(outw, neww_h, osem.at[1])
    store_w.start()

    for k in range(4):
        swap(k).wait_send()
        for kind in range(3):
            for way in range(2):
                hop(k, kind, way).wait_send()
        if k < 3:
            zhop(k).wait_send()

    def sent_one(i, carry):
        post(i).wait_send()
        return carry

    lax.fori_loop(1, N_REP, sent_one, 0)
    store_m.wait()
    store_w.wait()


def shards(activations, out_grad, momentum, weight, kept_tile):
    f32 = jnp.float32
    vm = pltpu.VMEM
    dma = pltpu.SemaphoreType.DMA
    return tuple(
        pl.pallas_call(
            kernel,
            out_shape=(
                jax.ShapeDtypeStruct(momentum.shape, f32),
                jax.ShapeDtypeStruct(weight.shape, f32),
            ),
            in_specs=[pl.BlockSpec(memory_space=pl.ANY)] * 6,
            out_specs=(pl.BlockSpec(memory_space=pl.ANY),) * 2,
            scratch_shapes=[
                vm((TOK, COLS), jnp.bfloat16),
                vm((TOK, TOK), jnp.bfloat16),
                vm((5, SPAN, SPAN), f32),
                vm((5, SPAN, SPAN), f32),
                pltpu.SMEM((1, 5), jnp.int32),
                vm((384, 128), f32),
                vm((2, N_ZLO, N_X, SLAB, 128), f32),
                vm((N_ZLO, N_X, SLAB, 128), f32),
                vm((4, 2, HALF, 128), f32),
                vm((4, 2, HALF, 128), f32),
                vm((4, 2, HALF, 128), f32),
                vm((3, SLAB, 128), f32),
                vm((N_REP, TILE, 128), f32),
                vm((5, SPAN, SPAN), f32),
                vm((5, SPAN, SPAN), f32),
                dma((7,)),
                dma((2,)),
                dma((4,)),
                dma((4,)),
                dma((24,)),
                dma((24,)),
                dma((3,)),
                dma((3,)),
                dma((N_REP,)),
                dma((N_REP,)),
            ],
            compiler_params=pltpu.CompilerParams(
                collective_id=0, has_side_effects=True, vmem_limit_bytes=62 * 1024 * 1024
            ),
            name="demo_step",
        )(activations, out_grad, momentum, weight, kept_tile, jnp.asarray(tables()))
    )


def solution(mesh):
    placed = (
        P(("rep", "fsdp"), None),
        P(("rep", "fsdp"), None),
        P("rep", "fsdp", None, None),
        P("fsdp", None, None),
        P("rep", "fsdp"),
    )
    return jax.shard_map(
        shards,
        mesh=mesh,
        in_specs=placed,
        out_specs=(P("rep", "fsdp", None, None), P("fsdp", None, None)),
        check_vma=False,
    )
```

time: 246 us -> 50.2 us (0.20)
  the two profiles are of different devices: /device:TPU:1 before, /device:TPU:2 now
where the time goes in v1:
time: 50.2 us; the launch traced here: 50 us
  Pallas kernels  46.2 us (92%)
  local copies, waits for them, and re-layouts  3.19 us (6%)
  between operations  0.64 us (1%)
    pallas_call x1, Pallas kernels, shards(): pl.pallas_call(kernel, out_shape=(jax.ShapeDtypeStruct(momentum.shape, f3...  46.2 us
    unnamed x2, local copies, waits for them, and re-layouts  3.19 us

profile of v1, /device:TPU:2, one launch (start us, length us, event | category | flops | bytes accessed | tf_op | source)
XLA Modules:
  0.0 50.0 jit_solution(9954432014314020602)
XLA Ops:
  0.6 46.2 %demo_step.1 = (f32[1,5,64,64]{3,2,1,0:T(8,128)}, f32[5,64,64]{2,1,0:T(8,128)}) custom-call(bf16[128,5120]{1,0:T(8,128)(2,1)} %acts_h.1, bf16[128,128]{1,0:T(8,128)(2,1)} %outg_h.1, f32[1,5,64,64]{3,2,1,0:T(8,128)} %mom_h.1, f32[5,64,64]{2,1,0:T(8,128)} %wt_h.1, s32[1,5]{1,0:T(1,128)} %kept_h.1, f32[384,128]{1,0:T(8,128)} %constant.2.clone.cst_h), custom_call_target="tpu_custom_call" | custom-call | tf_op jit(solution)/shard_map/demo_step/pallas_call | solution.py:347
  46.8 1.6 %copy.10 = f32[1,5,64,64]{3,2,1,0:T(8,128)} copy(f32[1,5,64,64]{3,2,1,0:T(8,128)} %get-tuple-element.4) | data formatting | bytes 163840
  48.4 1.6 %copy.11 = f32[5,64,64]{2,1,0:T(8,128)} copy(f32[5,64,64]{2,1,0:T(8,128)} %get-tuple-element.5) | data formatting | bytes 163840

commit v2 on v1

v2 whole, which is shorter than its diff:
```python
import jax
import jax.numpy as jnp
import ml_dtypes
import numpy as np
from jax import lax
from jax.experimental import pallas as pl
from jax.experimental.pallas import tpu as pltpu
from jax.sharding import PartitionSpec as P

SPAN = 64
TILE = 8
N_X = 4
N_ZLO = 4
N_REP = 16
SLAB = 160
HALF = SLAB // 2
TOK = 128
COLS = 5120
WIDE = 640
PARITY = 4 * WIDE

decay_rate = 0.9
step_size = 0.5
epsilon = 1e-06

MESH = pl.DeviceIdType.MESH


def tables():
    u = np.arange(SPAN, dtype=np.float64)[:, None]
    x = np.arange(SPAN, dtype=np.float64)[None, :]
    s = np.where(u == 0, np.sqrt(1.0 / SPAN), np.sqrt(2.0 / SPAN))
    basis = s * np.cos(np.pi * (2.0 * x + 1.0) * u / (2.0 * SPAN))
    zero = np.zeros((SPAN, SPAN))

    def halves(table):
        high = table.astype(ml_dtypes.bfloat16)
        return high, (table - high.astype(np.float64)).astype(ml_dtypes.bfloat16)

    def for_left(table):
        high, low = halves(np.concatenate([table, zero], 1))
        high, low = high[:, :SPAN], low[:, :SPAN]
        return np.concatenate([high, high, low, zero.astype(high.dtype)], 1)

    def for_right(table):
        high, low = halves(np.block([[table, zero], [zero, table]]))
        return np.concatenate([high, high, low], 0)

    lefts = np.concatenate([for_left(basis), for_left(basis.T)], 0)
    rights = np.concatenate([for_right(basis.T), for_right(basis)], 0)
    return lefts.astype(np.float32), rights.astype(np.float32)


def halve(a):
    high = a.astype(jnp.bfloat16)
    return high, (a - high.astype(jnp.float32)).astype(jnp.bfloat16)


def left(table, parts):
    high, low = halve(jnp.concatenate(parts, axis=1))
    data = jnp.concatenate([high, low, high], axis=0)
    wide = jnp.dot(table, data, preferred_element_type=jnp.float32)
    return [wide[:, 128 * p : 128 * p + 128] for p in range(3)]


def right(parts, table):
    high, low = halve(jnp.concatenate(parts, axis=0))
    data = jnp.concatenate([high, low, high], axis=1)
    tall = jnp.dot(data, table, preferred_element_type=jnp.float32)
    return [tall[SPAN * p : SPAN * p + SPAN] for p in range(3)]


def kernel(
    acts_h, outg_h, mom_h, wt_h, kept_h, lefts_h, rights_h,
    outm, outw,
    acts, outg, mom, wt, kept, lefts32, rights32, lefts, rights,
    part, rx, x1, x0, x2, zr, every,
    lsem, csend, crecv, xsend, xrecv, zsend, zrecv, gsend, grecv,
):
    rep = lax.axis_index("rep")
    f = lax.axis_index("fsdp")
    core = lax.rem(f, 2)
    x = lax.rem(f // 2, N_X)
    z = f // (2 * N_X)
    other = 1 - core
    xr, xl, xo = lax.rem(x + 1, N_X), lax.rem(x + 3, N_X), lax.rem(x + 2, N_X)

    def at(z_, x_, core_):
        return (rep, (z_ * N_X + x_) * 2 + core_)

    piece = [lax.rem(z + d, N_ZLO) for d in (1, 3, 2)] + [z]

    first = lax.rem(z + 1, 2)
    load_acts = []
    for k in range(2):
        par = first if k == 0 else 1 - first
        cols = pl.ds(pl.multiple_of(par * PARITY, 128), PARITY)
        load_acts.append(pltpu.make_async_copy(acts_h.at[:, cols], acts.at[:, cols], lsem.at[k]))
    load_outg = pltpu.make_async_copy(outg_h, outg, lsem.at[2])
    load_outg.start()
    load_acts[0].start()
    load_acts[1].start()
    small = [
        pltpu.make_async_copy(src, dst, lsem.at[3 + i])
        for i, (src, dst) in enumerate(((mom_h.at[0], mom), (wt_h, wt), (kept_h, kept), (lefts_h, lefts32), (rights_h, rights32)))
    ]
    for copy in small:
        copy.start()

    barrier = pltpu.get_barrier_semaphore()
    near = [at(z, x, other), at(z, xr, core), at(z, xl, core)] + [at(piece[k], x, core) for k in range(3)]
    for peer in near:
        pl.semaphore_signal(barrier, inc=1, device_id=peer, device_id_type=MESH)

    def greet(i, carry):
        pl.semaphore_signal(
            barrier, inc=1, device_id=(lax.rem(rep + i, N_REP), f), device_id_type=MESH
        )
        return carry

    lax.fori_loop(1, N_REP, greet, 0)

    lane = lax.broadcasted_iota(jnp.int32, (32, 128), 1)

    owners = [xo, xr, xl, x]

    def chunk(half, o, grads):
        par, j = (first if half == 0 else 1 - first), owners[o]
        base = pl.multiple_of(par * PARITY + j * WIDE, 128)
        prod = jnp.dot(grads, acts[:, pl.ds(base, WIDE)], preferred_element_type=jnp.float32)
        for h in range(2):
            blk = prod[SPAN * h : SPAN * h + SPAN]
            zz = 2 * h + par
            b2 = blk[:, 256:384]
            part[0, zz, j, 0:64] = blk[:, 0:128]
            part[0, zz, j, 64:128] = blk[:, 128:256]
            part[0, zz, j, 128:160] = jnp.where(lane < 64, b2[0:32], pltpu.roll(b2[32:64], 64, 1))
            part[1, zz, j, 0:64] = blk[:, 384:512]
            part[1, zz, j, 64:128] = blk[:, 512:640]
            part[1, zz, j, 128:160] = jnp.where(lane < 64, pltpu.roll(b2[0:32], 64, 1), b2[32:64])
        for k in (2 * half, 2 * half + 1):
            swap(k, o).start()

    def swap(k, o):
        return pltpu.make_async_remote_copy(
            src_ref=part.at[other, piece[k], owners[o]], dst_ref=rx.at[k, o],
            send_sem=csend.at[4 * k + o], recv_sem=crecv.at[4 * k + o],
            device_id=at(z, x, other), device_id_type=MESH,
        )

    A, B = pl.ds(0, HALF), pl.ds(HALF, HALF)

    def hop(k, kind, way):
        side = xr if way == 0 else xl
        slab = xo if kind == 1 else side
        rows = (B if way == 0 else A) if kind == 0 else (A if way == 0 else B)
        land = (x0, x1, x2)[kind]
        i = (k * 3 + kind) * 2 + way
        return pltpu.make_async_remote_copy(
            src_ref=part.at[core, piece[k], slab, rows], dst_ref=land.at[k, way],
            send_sem=xsend.at[i], recv_sem=xrecv.at[i],
            device_id=at(z, side, core), device_id_type=MESH,
        )

    def zhop(k):
        return pltpu.make_async_remote_copy(
            src_ref=part.at[core, piece[k], x], dst_ref=zr.at[k],
            send_sem=zsend.at[k], recv_sem=zrecv.at[k],
            device_id=at(piece[k], x, core), device_id_type=MESH,
        )

    def take(k, o):
        swap(k, o).wait_recv()
        slab = owners[o]
        part[core, piece[k], slab] = part[core, piece[k], slab] + rx[k, o]

    def open_far(k):
        take(k, 0)
        hop(k, 1, 0).start()
        hop(k, 1, 1).start()

    def open_near(k):
        for way in range(2):
            take(k, 1 + way)
            hop(k, 0, way).start()

    def pass_on(k):
        for way in range(2):
            hop(k, 1, way).wait_recv()
            side, rows = (xr, A) if way == 0 else (xl, B)
            part[core, piece[k], side, rows] = part[core, piece[k], side, rows] + x1[k, way]
            hop(k, 2, way).start()

    def close_piece(k):
        take(k, 3)
        for way in range(2):
            hop(k, 0, way).wait_recv()
            hop(k, 2, way).wait_recv()
        part[core, piece[k], x, A] = part[core, piece[k], x, A] + (x0[k, 1] + x2[k, 0])
        part[core, piece[k], x, B] = part[core, piece[k], x, B] + (x0[k, 0] + x2[k, 1])
        if k < 3:
            zhop(k).start()

    load_outg.wait()
    grads = outg[...].astype(jnp.float32).T.astype(jnp.bfloat16)
    load_acts[0].wait()
    pl.semaphore_wait(barrier, len(near) + N_REP - 1)
    chunk(0, 0, grads)
    chunk(0, 1, grads)
    chunk(0, 2, grads)
    open_far(0)
    open_far(1)
    chunk(0, 3, grads)
    open_near(0)
    open_near(1)
    load_acts[1].wait()
    chunk(1, 0, grads)
    pass_on(0)
    chunk(1, 1, grads)
    chunk(1, 2, grads)
    open_far(2)
    pass_on(1)
    open_far(3)
    chunk(1, 3, grads)
    open_near(2)
    close_piece(0)
    close_piece(1)
    pass_on(2)
    open_near(3)
    pass_on(3)
    close_piece(2)

    for copy in small:
        copy.wait()
    lefts[...] = lefts32[...].astype(jnp.bfloat16)
    rights[...] = rights32[...].astype(jnp.bfloat16)
    order = [core, core + 1, core + 2, core + 3, 4 * other]
    numbers = [kept[0, s] for s in order]
    wide = lax.broadcasted_iota(jnp.int32, (SPAN, 128), 1)
    row = lax.broadcasted_iota(jnp.int32, (SPAN, 128), 0)
    place = (row // TILE) * TILE + lax.rem(wide, SPAN) // TILE

    def pairs(ref):
        zero = jnp.zeros((SPAN, SPAN), jnp.float32)
        return [
            jnp.concatenate([ref[order[0]], ref[order[1]]], axis=1),
            jnp.concatenate([ref[order[2]], ref[order[3]]], axis=1),
            jnp.concatenate([ref[order[4]], zero], axis=1),
        ]

    def unpair(ref, parts):
        for j in range(5):
            half = parts[j // 2][:, SPAN * (j % 2) : SPAN * (j % 2) + SPAN]
            ref[order[j]] = half

    carried = [decay_rate * m for m in pairs(mom)]
    keep = [
        place == jnp.where(wide < SPAN, numbers[2 * p], numbers[min(2 * p + 1, 4)]) for p in range(3)
    ]
    fwd_l, inv_l = lefts[0:64, 0:192], lefts[64:128, 0:192]
    fwd_r, inv_r = rights[0:384], rights[384:768]

    close_piece(3)
    for k in range(3):
        zhop(k).wait_recv()
    total = part[core, z, x] + (zr[0] + zr[1] + zr[2])
    tail = jnp.concatenate([total[128:160], pltpu.roll(total[128:160], 64, 1)], axis=0)
    state = [
        carried[0] + total[0:64],
        carried[1] + total[64:128],
        carried[2] + jnp.where(wide < SPAN, tail, 0.0),
    ]
    coef = right(left(fwd_l, state), fwd_r)
    kept_coef = [jnp.where(keep[p], coef[p], 0.0) for p in range(3)]

    lane8 = lax.broadcasted_iota(jnp.int32, (TILE, 128), 1)
    message = jnp.zeros((TILE, 128), jnp.float32)
    for j in range(5):
        tile = jnp.sum(kept_coef[j // 2].reshape(8, TILE, 128), axis=0)
        tile = jnp.where((lane8 < SPAN) == (j % 2 == 0), tile, 0.0)
        for shift in (8, 16, 32, 64):
            tile = tile + pltpu.roll(tile, shift, 1)
        message = jnp.where(lax.rem(lane8, SPAN) // TILE == j, tile, message)
        message = jnp.where(lax.rem(lane8, SPAN) == 40 + j, numbers[j].astype(jnp.float32), message)
    every[rep] = jnp.where(lane8[0:4] < SPAN, message[0:4], message[4:8])

    def post(i):
        return pltpu.make_async_remote_copy(
            src_ref=every.at[rep], dst_ref=every.at[rep],
            send_sem=gsend, recv_sem=grecv,
            device_id=(lax.rem(rep + i, N_REP), f), device_id_type=MESH,
        )

    def all_posts():
        span = pl.ds(0, N_REP - 1)
        return pltpu.make_async_remote_copy(
            src_ref=every.at[span], dst_ref=every.at[span], send_sem=gsend, recv_sem=grecv,
            device_id=(lax.rem(rep + 1, N_REP), f), device_id_type=MESH,
        )

    def send_one(i, carry):
        post(i).start()
        return carry

    lax.fori_loop(1, N_REP, send_one, 0)

    decoded = left(inv_l, right(kept_coef, inv_r))
    unpair(outm.at[0], [state[p] - decoded[p] for p in range(3)])
    weights = pairs(wt)

    for k in range(4):
        for o in range(4):
            swap(k, o).wait_send()
        for kind in range(3):
            for way in range(2):
                hop(k, kind, way).wait_send()
        if k < 3:
            zhop(k).wait_send()
    all_posts().wait_send()
    all_posts().wait_recv()

    src_tile = [8 * jnp.where(lane8 < SPAN, 2 * p, min(2 * p + 1, 4)) + lax.rem(lane8, 8) for p in range(3)]
    src_num = [40 + jnp.where(lane8 < SPAN, 2 * p, min(2 * p + 1, 4)) for p in range(3)]
    place_f = place.astype(jnp.float32).reshape(8, TILE, 128)

    def gather_one(g, sums):
        got = every[g]
        got = jnp.concatenate([got, pltpu.roll(got, SPAN, 1)], axis=0)
        new = []
        for p in range(3):
            tile = jnp.take_along_axis(got, src_tile[p], axis=1)
            num = jnp.take_along_axis(got, src_num[p], axis=1)
            new.append(sums[p] + jnp.where(num[None] == place_f, tile[None], 0.0))
        return tuple(new)

    sums = lax.fori_loop(
        0, N_REP, gather_one, tuple(jnp.zeros((8, TILE, 128), jnp.float32) for _ in range(3)),
        unroll=True,
    )
    update = left(inv_l, right([s.reshape(SPAN, 128) for s in sums], inv_r))
    fresh = []
    for p in range(3):
        square = jnp.sum(update[p] * update[p], axis=0, keepdims=True)
        low = wide[0:1] < SPAN
        mean_lo = jnp.sum(jnp.where(low, square, 0.0), axis=1, keepdims=True) / (SPAN * SPAN)
        mean_hi = jnp.sum(jnp.where(low, 0.0, square), axis=1, keepdims=True) / (SPAN * SPAN)
        spread = jnp.sqrt(jnp.where(low, mean_lo, mean_hi) + epsilon)
        fresh.append(weights[p] - step_size * update[p] / spread)
    unpair(outw, fresh)


def shards(activations, out_grad, momentum, weight, kept_tile):
    f32 = jnp.float32
    vm = pltpu.VMEM
    dma = pltpu.SemaphoreType.DMA
    return tuple(
        pl.pallas_call(
            kernel,
            out_shape=(
                pltpu.VMEM(momentum.shape, f32),
                pltpu.VMEM(weight.shape, f32),
            ),
            in_specs=[pl.BlockSpec(memory_space=pltpu.HBM)] * 7,
            out_specs=(pl.BlockSpec(memory_space=pltpu.VMEM),) * 2,
            scratch_shapes=[
                vm((TOK, COLS), jnp.bfloat16),
                vm((TOK, TOK), jnp.bfloat16),
                vm((5, SPAN, SPAN), f32),
                vm((5, SPAN, SPAN), f32),
                pltpu.SMEM((1, 5), jnp.int32),
                vm((128, 256), f32),
                vm((768, 128), f32),
                vm((128, 256), jnp.bfloat16),
                vm((768, 128), jnp.bfloat16),
                vm((2, N_ZLO, N_X, SLAB, 128), f32),
                vm((N_ZLO, N_X, SLAB, 128), f32),
                vm((4, 2, HALF, 128), f32),
                vm((4, 2, HALF, 128), f32),
                vm((4, 2, HALF, 128), f32),
                vm((3, SLAB, 128), f32),
                vm((N_REP, TILE // 2, 128), f32),
                dma((8,)),
                dma((16,)),
                dma((16,)),
                dma((24,)),
                dma((24,)),
                dma((3,)),
                dma((3,)),
                dma,
                dma,
            ],
            compiler_params=pltpu.CompilerParams(
                collective_id=0, has_side_effects=True, vmem_limit_bytes=48 * 1024 * 1024
            ),
            name="demo_step",
        )(*(
            pltpu.with_memory_space_constraint(a, pltpu.HBM)
            for a in (activations, out_grad, momentum, weight, kept_tile, *map(jnp.asarray, tables()))
        ))
    )


def solution(mesh):
    placed = (
        P(("rep", "fsdp"), None),
        P(("rep", "fsdp"), None),
        P("rep", "fsdp", None, None),
        P("fsdp", None, None),
        P("rep", "fsdp"),
    )
    return jax.shard_map(
        shards,
        mesh=mesh,
        in_specs=placed,
        out_specs=(P("rep", "fsdp", None, None), P("fsdp", None, None)),
        check_vma=False,
    )
```

time: 50.2 us -> 46 us (0.916)
  the two profiles are of different devices: /device:TPU:2 before, /device:TPU:8 now
where the time goes in v2:
time: 46 us; the launch traced here: 45.9 us
  Pallas kernels  43.9 us (95%)
  local copies, waits for them, and re-layouts  1.33 us (3%)
  between operations  0.64 us (1%)
    pallas_call x1, Pallas kernels, shards(): pl.pallas_call(kernel, out_shape=(pltpu.VMEM(momentum.shape, f32), pltpu....  43.9 us
    unnamed x2, local copies, waits for them, and re-layouts  1.33 us

profile of v2, /device:TPU:8, one launch (start us, length us, event | category | flops | bytes accessed | tf_op | source)
XLA Modules:
  0.0 45.9 jit_solution(16410143621531412637)
XLA Ops:
  0.6 43.9 %demo_step.1 = (f32[1,5,64,64]{3,2,1,0:T(8,128)S(1)}, f32[5,64,64]{2,1,0:T(8,128)S(1)}) custom-call(bf16[128,5120]{1,0:T(8,128)(2,1)} %acts_h.1, bf16[128,128]{1,0:T(8,128)(2,1)} %outg_h.1, f32[1,5,64,64]{3,2,1,0:T(8,128)} %mom_h.1, f32[5,64,64]{2,1,0:T(8,128)} %wt_h.1, s32[1,5]{1,0:T(1,128)} %kept_h.1, f32[128,256]{1,0:T(8,128)} %constant.4.clone.lefts_h, ...), custom_call_target="tpu_custom_call" | custom-call | tf_op jit(solution)/shard_map/demo_step/pallas_call | solution.py:357
  44.5 0.7 %copy.11 = f32[1,5,64,64]{3,2,1,0:T(8,128)} copy(f32[1,5,64,64]{3,2,1,0:T(8,128)S(1)} %get-tuple-element.2) | data formatting | bytes 163840
  45.2 0.7 %copy.12 = f32[5,64,64]{2,1,0:T(8,128)} copy(f32[5,64,64]{2,1,0:T(8,128)S(1)} %get-tuple-element.3) | data formatting | bytes 163840

commit v3 on v2

--- a/solution.py
+++ b/solution.py
@@ -12,6 +12,7 @@
 N_X = 4
 N_ZLO = 4
 N_REP = 16
+N_FSDP = 32
 SLAB = 160
 HALF = SLAB // 2
 TOK = 128
@@ -74,8 +75,8 @@
     acts_h, outg_h, mom_h, wt_h, kept_h, lefts_h, rights_h,
     outm, outw,
     acts, outg, mom, wt, kept, lefts32, rights32, lefts, rights,
-    part, rx, x1, x0, x2, zr, every,
-    lsem, csend, crecv, xsend, xrecv, zsend, zrecv, gsend, grecv,
+    part, rx, x1, x0, x2, zr, turned, names, tmsg, tin, every,
+    lsem, csend, crecv, xsend, xrecv, zsend, zrecv, nsend, nrecv, tsend, trecv, gsend, grecv,
 ):
     rep = lax.axis_index("rep")
     f = lax.axis_index("fsdp")
@@ -108,17 +109,21 @@
         copy.start()
 
     barrier = pltpu.get_barrier_semaphore()
-    near = [at(z, x, other), at(z, xr, core), at(z, xl, core)] + [at(piece[k], x, core) for k in range(3)]
-    for peer in near:
-        pl.semaphore_signal(barrier, inc=1, device_id=peer, device_id_type=MESH)
-
-    def greet(i, carry):
+
+    def greet_group(i, carry):
+        pl.semaphore_signal(
+            barrier, inc=1, device_id=(rep, lax.rem(f + i, N_FSDP)), device_id_type=MESH
+        )
+        return carry
+
+    def greet_peers(i, carry):
         pl.semaphore_signal(
             barrier, inc=1, device_id=(lax.rem(rep + i, N_REP), f), device_id_type=MESH
         )
         return carry
 
-    lax.fori_loop(1, N_REP, greet, 0)
+    lax.fori_loop(1, N_FSDP, greet_group, 0)
+    lax.fori_loop(1, N_REP, greet_peers, 0)
 
     lane = lax.broadcasted_iota(jnp.int32, (32, 128), 1)
 
@@ -201,10 +206,122 @@
         if k < 3:
             zhop(k).start()
 
+    order = [core, core + 1, core + 2, core + 3, 4 * other]
+    lane1 = lax.broadcasted_iota(jnp.int32, (1, 128), 1)
+    lane4 = lax.broadcasted_iota(jnp.int32, (4, 128), 1)
+    lane8 = lax.broadcasted_iota(jnp.int32, (TILE, 128), 1)
+    wide = lax.broadcasted_iota(jnp.int32, (SPAN, 128), 1)
+    row = lax.broadcasted_iota(jnp.int32, (SPAN, 128), 0)
+    place = (row // TILE) * TILE + lax.rem(wide, SPAN) // TILE
+    upper = jnp.where(lane8 < SPAN, 0, SPAN)
+    block = lax.rem(lane8, SPAN) // TILE
+
+    def to_group(src, dst, send, recv, i):
+        return pltpu.make_async_remote_copy(
+            src_ref=src, dst_ref=dst, send_sem=send, recv_sem=recv,
+            device_id=(rep, lax.rem(f + i, N_FSDP)), device_id_type=MESH,
+        )
+
+    def to_peer(src, dst, send, recv, i):
+        return pltpu.make_async_remote_copy(
+            src_ref=src, dst_ref=dst, send_sem=send, recv_sem=recv,
+            device_id=(lax.rem(rep + i, N_REP), f), device_id_type=MESH,
+        )
+
+    def send_names():
+        mine = jnp.zeros((1, 128), jnp.int32)
+        for s in range(5):
+            mine = jnp.where(lane1 == s, kept[0, s], mine)
+        names[f] = mine
+
+        def one(i, carry):
+            to_group(names.at[f], names.at[f], nsend, nrecv, i).start()
+            return carry
+
+        lax.fori_loop(1, N_FSDP, one, 0)
+
+    def all_names():
+        ref = names.at[pl.ds(0, N_FSDP - 1)]
+        return to_group(ref, ref, nsend, nrecv, 1)
+
+    def pick_columns(tile, number):
+        source = (number & 7) * TILE + lax.rem(lane8, TILE) + upper
+        return jnp.take_along_axis(tile, source, axis=1)
+
+    def merge(a, b, c):
+        return jnp.where(block == 0, a, jnp.where(block == 1, b, c))
+
+    def pack(tiles):
+        return jnp.where(lax.rem(lane4, SPAN) < 24, tiles[0:4], pltpu.roll(tiles[4:8], 24, 1))
+
+    def unpack(four):
+        return jnp.concatenate([four, pltpu.roll(four, 104, 1)], axis=0)
+
+    def group_tiles(m, carry):
+        base = pl.multiple_of(m * WIDE, 128)
+        both = jnp.dot(turned[...], acts[:, pl.ds(base, WIDE)], preferred_element_type=jnp.float32)
+        both = both[0:128] + both[128:256]
+        numbers, rows = [], []
+        for h in range(2):
+            owner = ((2 * h + m // 4) * N_X + lax.rem(m, 4)) * 2
+            low = jnp.broadcast_to(names[owner], (TILE, 128))
+            high = jnp.broadcast_to(names[owner + 1], (TILE, 128))
+            ten = jnp.where(lane8 < 5, low, pltpu.roll(high, 5, 1))
+            for p in range(5):
+                number = jnp.take_along_axis(ten, jnp.where(lane8 < SPAN, 2 * p, 2 * p + 1), axis=1)
+                high_part = number >> 3
+                found = jnp.zeros((TILE, 128), jnp.float32)
+                for a in range(8):
+                    at_row = SPAN * h + TILE * a
+                    found = found + jnp.where(
+                        high_part == a, both[at_row : at_row + TILE, 128 * p : 128 * p + 128], 0.0
+                    )
+                numbers.append(number)
+                rows.append(found)
+        high, low = halve(jnp.concatenate(rows, axis=0))
+        data = jnp.concatenate([high, low, high], axis=1)
+        turned_rows = jnp.dot(data, rights[0:384], preferred_element_type=jnp.float32)
+        for h in range(2):
+            owner = ((2 * h + m // 4) * N_X + lax.rem(m, 4)) * 2
+            t = [
+                pick_columns(turned_rows[TILE * q : TILE * q + TILE], numbers[q])
+                for q in range(5 * h, 5 * h + 5)
+            ]
+            tmsg[owner] = pack(merge(t[0], t[1], t[2]))
+            tmsg[owner + 1] = pack(merge(t[3], t[4], pltpu.roll(t[2], SPAN, 1)))
+        return carry
+
+    def send_tiles():
+        tin[f] = tmsg[f]
+
+        def one(i, carry):
+            to_group(tmsg.at[lax.rem(f + i, N_FSDP)], tin.at[f], tsend, trecv, i).start()
+            return carry
+
+        lax.fori_loop(1, N_FSDP, one, 0)
+
+    def all_tiles():
+        span = pl.ds(0, N_FSDP - 1)
+        return to_group(tmsg.at[span], tin.at[span], tsend, trecv, 1)
+
+    def pairs(ref):
+        zero = jnp.zeros((SPAN, SPAN), jnp.float32)
+        return [
+            jnp.concatenate([ref[order[0]], ref[order[1]]], axis=1),
+            jnp.concatenate([ref[order[2]], ref[order[3]]], axis=1),
+            jnp.concatenate([ref[order[4]], zero], axis=1),
+        ]
+
+    def unpair(ref, parts):
+        for j in range(5):
+            half = parts[j // 2][:, SPAN * (j % 2) : SPAN * (j % 2) + SPAN]
+            ref[order[j]] = half
+
     load_outg.wait()
-    grads = outg[...].astype(jnp.float32).T.astype(jnp.bfloat16)
+    flat = outg[...]
+    grads = flat.astype(jnp.float32).T.astype(jnp.bfloat16)
     load_acts[0].wait()
-    pl.semaphore_wait(barrier, len(near) + N_REP - 1)
+    pl.semaphore_wait(barrier, N_FSDP - 1 + N_REP - 1)
     chunk(0, 0, grads)
     chunk(0, 1, grads)
     chunk(0, 2, grads)
@@ -213,6 +330,9 @@
     chunk(0, 3, grads)
     open_near(0)
     open_near(1)
+    for copy in small:
+        copy.wait()
+    send_names()
     load_acts[1].wait()
     chunk(1, 0, grads)
     pass_on(0)
@@ -223,109 +343,83 @@
     open_far(3)
     chunk(1, 3, grads)
     open_near(2)
-    close_piece(0)
-    close_piece(1)
-    pass_on(2)
-    open_near(3)
-    pass_on(3)
-    close_piece(2)
-
-    for copy in small:
-        copy.wait()
+
     lefts[...] = lefts32[...].astype(jnp.bfloat16)
     rights[...] = rights32[...].astype(jnp.bfloat16)
-    order = [core, core + 1, core + 2, core + 3, 4 * other]
-    numbers = [kept[0, s] for s in order]
-    wide = lax.broadcasted_iota(jnp.int32, (SPAN, 128), 1)
-    row = lax.broadcasted_iota(jnp.int32, (SPAN, 128), 0)
-    place = (row // TILE) * TILE + lax.rem(wide, SPAN) // TILE
-
-    def pairs(ref):
-        zero = jnp.zeros((SPAN, SPAN), jnp.float32)
-        return [
-            jnp.concatenate([ref[order[0]], ref[order[1]]], axis=1),
-            jnp.concatenate([ref[order[2]], ref[order[3]]], axis=1),
-            jnp.concatenate([ref[order[4]], zero], axis=1),
-        ]
-
-    def unpair(ref, parts):
-        for j in range(5):
-            half = parts[j // 2][:, SPAN * (j % 2) : SPAN * (j % 2) + SPAN]
-            ref[order[j]] = half
-
-    carried = [decay_rate * m for m in pairs(mom)]
-    keep = [
-        place == jnp.where(wide < SPAN, numbers[2 * p], numbers[min(2 * p + 1, 4)]) for p in range(3)
-    ]
     fwd_l, inv_l = lefts[0:64, 0:192], lefts[64:128, 0:192]
     fwd_r, inv_r = rights[0:384], rights[384:768]
-
-    close_piece(3)
-    for k in range(3):
-        zhop(k).wait_recv()
-    total = part[core, z, x] + (zr[0] + zr[1] + zr[2])
-    tail = jnp.concatenate([total[128:160], pltpu.roll(total[128:160], 64, 1)], axis=0)
-    state = [
-        carried[0] + total[0:64],
-        carried[1] + total[64:128],
-        carried[2] + jnp.where(wide < SPAN, tail, 0.0),
+    spun = jnp.dot(flat, rights[0:128], preferred_element_type=jnp.float32)
+    spun = spun + jnp.dot(flat, rights[256:384], preferred_element_type=jnp.float32)
+    spun_high, spun_low = halve(spun.T)
+    turned[0:128] = spun_high
+    turned[128:256] = spun_low
+    open_near(3)
+    all_names().wait_recv()
+    lax.fori_loop(0, 4, group_tiles, 0)
+    close_piece(0)
+    pass_on(2)
+    lax.fori_loop(4, 8, group_tiles, 0)
+    pass_on(3)
+    close_piece(1)
+    send_tiles()
+
+    scalars = [kept[0, s] for s in order]
+    carried = [decay_rate * m for m in pairs(mom)]
+    own = [
+        jnp.where(wide < SPAN, scalars[2 * p], scalars[min(2 * p + 1, 4)]) for p in range(3)
     ]
-    coef = right(left(fwd_l, state), fwd_r)
-    kept_coef = [jnp.where(keep[p], coef[p], 0.0) for p in range(3)]
-
-    lane8 = lax.broadcasted_iota(jnp.int32, (TILE, 128), 1)
-    message = jnp.zeros((TILE, 128), jnp.float32)
+    coef = right(left(fwd_l, carried), fwd_r)
+    found = [
+        pick_columns(
+            jnp.sum(jnp.where(place == own[p], coef[p], 0.0).reshape(8, TILE, 128), axis=0), own[p][0:8]
+        )
+        for p in range(3)
+    ]
+    from_momentum = merge(*found)
+    close_piece(2)
+
+    all_tiles().wait_recv()
+    tiles = from_momentum + unpack(jnp.sum(tin[...], axis=0))
+    message = pack(tiles)
     for j in range(5):
-        tile = jnp.sum(kept_coef[j // 2].reshape(8, TILE, 128), axis=0)
-        tile = jnp.where((lane8 < SPAN) == (j % 2 == 0), tile, 0.0)
-        for shift in (8, 16, 32, 64):
-            tile = tile + pltpu.roll(tile, shift, 1)
-        message = jnp.where(lax.rem(lane8, SPAN) // TILE == j, tile, message)
-        message = jnp.where(lax.rem(lane8, SPAN) == 40 + j, numbers[j].astype(jnp.float32), message)
-    every[rep] = jnp.where(lane8[0:4] < SPAN, message[0:4], message[4:8])
-
-    def post(i):
-        return pltpu.make_async_remote_copy(
-            src_ref=every.at[rep], dst_ref=every.at[rep],
-            send_sem=gsend, recv_sem=grecv,
-            device_id=(lax.rem(rep + i, N_REP), f), device_id_type=MESH,
-        )
+        spot = (lane4 == 56 + j) | (lane4 == 80 + j)
+        message = jnp.where(spot, scalars[j].astype(jnp.float32), message)
+    every[rep] = message
+
+    def send_one(i, carry):
+        to_peer(every.at[rep], every.at[rep], gsend, grecv, i).start()
+        return carry
+
+    lax.fori_loop(1, N_REP, send_one, 0)
 
     def all_posts():
-        span = pl.ds(0, N_REP - 1)
-        return pltpu.make_async_remote_copy(
-            src_ref=every.at[span], dst_ref=every.at[span], send_sem=gsend, recv_sem=grecv,
-            device_id=(lax.rem(rep + 1, N_REP), f), device_id_type=MESH,
-        )
-
-    def send_one(i, carry):
-        post(i).start()
-        return carry
-
-    lax.fori_loop(1, N_REP, send_one, 0)
-
-    decoded = left(inv_l, right(kept_coef, inv_r))
-    unpair(outm.at[0], [state[p] - decoded[p] for p in range(3)])
+        ref = every.at[pl.ds(0, N_REP - 1)]
+        return to_peer(ref, ref, gsend, grecv, 1)
+
+    src_tile = [upper + TILE * p + lax.rem(lane8, TILE) for p in range(3)]
+    src_num = [56 + jnp.where(lane8 < SPAN, 2 * p, min(2 * p + 1, 4)) for p in range(3)]
+
+    def spread_out(p):
+        tile = jnp.take_along_axis(tiles, src_tile[p], axis=1)
+        tall = jnp.broadcast_to(tile[None], (8, TILE, 128)).reshape(SPAN, 128)
+        return jnp.where(place == own[p], tall, 0.0)
+
+    decoded = left(inv_l, right([spread_out(p) for p in range(3)], inv_r))
+    for p in range(3):
+        carried[p] = carried[p] - decoded[p]
     weights = pairs(wt)
-
     for k in range(4):
         for o in range(4):
             swap(k, o).wait_send()
-        for kind in range(3):
-            for way in range(2):
-                hop(k, kind, way).wait_send()
-        if k < 3:
-            zhop(k).wait_send()
+    all_names().wait_send()
+    all_tiles().wait_send()
     all_posts().wait_send()
     all_posts().wait_recv()
 
-    src_tile = [8 * jnp.where(lane8 < SPAN, 2 * p, min(2 * p + 1, 4)) + lax.rem(lane8, 8) for p in range(3)]
-    src_num = [40 + jnp.where(lane8 < SPAN, 2 * p, min(2 * p + 1, 4)) for p in range(3)]
     place_f = place.astype(jnp.float32).reshape(8, TILE, 128)
 
     def gather_one(g, sums):
-        got = every[g]
-        got = jnp.concatenate([got, pltpu.roll(got, SPAN, 1)], axis=0)
+        got = unpack(every[g])
         new = []
         for p in range(3):
             tile = jnp.take_along_axis(got, src_tile[p], axis=1)
@@ -347,6 +441,19 @@
         spread = jnp.sqrt(jnp.where(low, mean_lo, mean_hi) + epsilon)
         fresh.append(weights[p] - step_size * update[p] / spread)
     unpair(outw, fresh)
+
+    close_piece(3)
+    for k in range(4):
+        for kind in range(3):
+            for way in range(2):
+                hop(k, kind, way).wait_send()
+        if k < 3:
+            zhop(k).wait_send()
+    for k in range(3):
+        zhop(k).wait_recv()
+    total = part[core, z, x] + (zr[0] + zr[1] + zr[2])
+    tail = jnp.concatenate([total[128:160], pltpu.roll(total[128:160], 64, 1)], axis=0)
+    unpair(outm.at[0], [carried[0] + total[0:64], carried[1] + total[64:128], carried[2] + tail])
 
 
 def shards(activations, out_grad, momentum, weight, kept_tile):
@@ -378,6 +485,10 @@
                 vm((4, 2, HALF, 128), f32),
                 vm((4, 2, HALF, 128), f32),
                 vm((3, SLAB, 128), f32),
+                vm((2 * TOK, TOK), jnp.bfloat16),
+                vm((N_FSDP, 1, 128), jnp.int32),
+                vm((N_FSDP, TILE // 2, 128), f32),
+                vm((N_FSDP, TILE // 2, 128), f32),
                 vm((N_REP, TILE // 2, 128), f32),
                 dma((8,)),
                 dma((16,)),
@@ -386,6 +497,10 @@
                 dma((24,)),
                 dma((3,)),
                 dma((3,)),
+                dma,
+                dma,
+                dma,
+                dma,
                 dma,
                 dma,
             ],

time: 46 us -> 48.8 us (1.061)
  the two profiles are of different devices: /device:TPU:8 before, /device:TPU:1 now
where the time goes in v3:
time: 48.8 us; the launch traced here: 48.7 us
  Pallas kernels  46.7 us (96%)
  local copies, waits for them, and re-layouts  1.33 us (3%)
  between operations  0.64 us (1%)
    pallas_call x1, Pallas kernels, shards(): pl.pallas_call(kernel, out_shape=(pltpu.VMEM(momentum.shape, f32), pltpu....  46.7 us
    unnamed x2, local copies, waits for them, and re-layouts  1.33 us

profile of v3, /device:TPU:1, one launch (start us, length us, event | category | flops | bytes accessed | tf_op | source)
XLA Modules:
  0.0 48.7 jit_solution(6041263940059191812)
XLA Ops:
  0.6 46.7 %demo_step.1 = (f32[1,5,64,64]{3,2,1,0:T(8,128)S(1)}, f32[5,64,64]{2,1,0:T(8,128)S(1)}) custom-call(bf16[128,5120]{1,0:T(8,128)(2,1)} %acts_h.1, bf16[128,128]{1,0:T(8,128)(2,1)} %outg_h.1, f32[1,5,64,64]{3,2,1,0:T(8,128)} %mom_h.1, f32[5,64,64]{2,1,0:T(8,128)} %wt_h.1, s32[1,5]{1,0:T(1,128)} %kept_h.1, f32[128,256]{1,0:T(8,128)} %constant.4.clone.lefts_h, ...), custom_call_target="tpu_custom_call" | custom-call | tf_op jit(solution)/shard_map/demo_step/pallas_call | solution.py:464
  47.3 0.7 %copy.11 = f32[1,5,64,64]{3,2,1,0:T(8,128)} copy(f32[1,5,64,64]{3,2,1,0:T(8,128)S(1)} %get-tuple-element.2) | data formatting | bytes 163840
  48.0 0.7 %copy.12 = f32[5,64,64]{2,1,0:T(8,128)} copy(f32[5,64,64]{2,1,0:T(8,128)S(1)} %get-tuple-element.3) | data formatting | bytes 163840

commit v4 on v3

--- a/solution.py
+++ b/solution.py
@@ -69,6 +69,10 @@
     data = jnp.concatenate([high, low, high], axis=1)
     tall = jnp.dot(data, table, preferred_element_type=jnp.float32)
     return [tall[SPAN * p : SPAN * p + SPAN] for p in range(3)]
+
+
+def wrap(i, n):
+    return jnp.where(i >= n, i - n, i)
 
 
 def kernel(
@@ -112,13 +116,13 @@
 
     def greet_group(i, carry):
         pl.semaphore_signal(
-            barrier, inc=1, device_id=(rep, lax.rem(f + i, N_FSDP)), device_id_type=MESH
+            barrier, inc=1, device_id=(rep, wrap(f + i, N_FSDP)), device_id_type=MESH
         )
         return carry
 
     def greet_peers(i, carry):
         pl.semaphore_signal(
-            barrier, inc=1, device_id=(lax.rem(rep + i, N_REP), f), device_id_type=MESH
+            barrier, inc=1, device_id=(wrap(rep + i, N_REP), f), device_id_type=MESH
         )
         return carry
 
@@ -219,13 +223,13 @@
     def to_group(src, dst, send, recv, i):
         return pltpu.make_async_remote_copy(
             src_ref=src, dst_ref=dst, send_sem=send, recv_sem=recv,
-            device_id=(rep, lax.rem(f + i, N_FSDP)), device_id_type=MESH,
+            device_id=(rep, wrap(f + i, N_FSDP)), device_id_type=MESH,
         )
 
     def to_peer(src, dst, send, recv, i):
         return pltpu.make_async_remote_copy(
             src_ref=src, dst_ref=dst, send_sem=send, recv_sem=recv,
-            device_id=(lax.rem(rep + i, N_REP), f), device_id_type=MESH,
+            device_id=(wrap(rep + i, N_REP), f), device_id_type=MESH,
         )
 
     def send_names():
@@ -291,11 +295,15 @@
             tmsg[owner + 1] = pack(merge(t[3], t[4], pltpu.roll(t[2], SPAN, 1)))
         return carry
 
+    def two_chunks(i, carry):
+        group_tiles(2 * i, carry)
+        return group_tiles(2 * i + 1, carry)
+
     def send_tiles():
         tin[f] = tmsg[f]
 
         def one(i, carry):
-            to_group(tmsg.at[lax.rem(f + i, N_FSDP)], tin.at[f], tsend, trecv, i).start()
+            to_group(tmsg.at[wrap(f + i, N_FSDP)], tin.at[f], tsend, trecv, i).start()
             return carry
 
         lax.fori_loop(1, N_FSDP, one, 0)
@@ -355,13 +363,12 @@
     turned[128:256] = spun_low
     open_near(3)
     all_names().wait_recv()
-    lax.fori_loop(0, 4, group_tiles, 0)
+    lax.fori_loop(0, 2, two_chunks, 0)
+    pass_on(2)
+    lax.fori_loop(2, 4, two_chunks, 0)
+    send_tiles()
+    pass_on(3)
     close_piece(0)
-    pass_on(2)
-    lax.fori_loop(4, 8, group_tiles, 0)
-    pass_on(3)
-    close_piece(1)
-    send_tiles()
 
     scalars = [kept[0, s] for s in order]
     carried = [decay_rate * m for m in pairs(mom)]
@@ -376,7 +383,6 @@
         for p in range(3)
     ]
     from_momentum = merge(*found)
-    close_piece(2)
 
     all_tiles().wait_recv()
     tiles = from_momentum + unpack(jnp.sum(tin[...], axis=0))
@@ -396,6 +402,8 @@
         ref = every.at[pl.ds(0, N_REP - 1)]
         return to_peer(ref, ref, gsend, grecv, 1)
 
+    close_piece(1)
+    close_piece(2)
     src_tile = [upper + TILE * p + lax.rem(lane8, TILE) for p in range(3)]
     src_num = [56 + jnp.where(lane8 < SPAN, 2 * p, min(2 * p + 1, 4)) for p in range(3)]
 

time: 48.8 us -> 47.5 us (0.973)
  Pallas kernels: 46.7 us -> 45.4 us
    pallas_call x1, Pallas kernels: 46.7 us -> 45.4 us  [shards(): pl.pallas_call(kernel, out_shape=(pltpu.VMEM(momentum.shape, f32), pltpu....]
where the time goes in v4:
time: 47.5 us; the launch traced here: 47.4 us
  Pallas kernels  45.4 us (96%)
  local copies, waits for them, and re-layouts  1.33 us (3%)
  between operations  0.64 us (1%)
    pallas_call x1, Pallas kernels, shards(): pl.pallas_call(kernel, out_shape=(pltpu.VMEM(momentum.shape, f32), pltpu....  45.4 us
    unnamed x2, local copies, waits for them, and re-layouts  1.33 us

profile of v4, /device:TPU:1, one launch (start us, length us, event | category | flops | bytes accessed | tf_op | source)
XLA Modules:
  0.0 47.4 jit_solution(6071361659803494475)
XLA Ops:
  0.6 45.4 %demo_step.1 = (f32[1,5,64,64]{3,2,1,0:T(8,128)S(1)}, f32[5,64,64]{2,1,0:T(8,128)S(1)}) custom-call(bf16[128,5120]{1,0:T(8,128)(2,1)} %acts_h.1, bf16[128,128]{1,0:T(8,128)(2,1)} %outg_h.1, f32[1,5,64,64]{3,2,1,0:T(8,128)} %mom_h.1, f32[5,64,64]{2,1,0:T(8,128)} %wt_h.1, s32[1,5]{1,0:T(1,128)} %kept_h.1, f32[128,256]{1,0:T(8,128)} %constant.4.clone.lefts_h, ...), custom_call_target="tpu_custom_call" | custom-call | tf_op jit(solution)/shard_map/demo_step/pallas_call | solution.py:472
  46.0 0.7 %copy.11 = f32[1,5,64,64]{3,2,1,0:T(8,128)} copy(f32[1,5,64,64]{3,2,1,0:T(8,128)S(1)} %get-tuple-element.2) | data formatting | bytes 163840
  46.7 0.7 %copy.12 = f32[5,64,64]{2,1,0:T(8,128)} copy(f32[5,64,64]{2,1,0:T(8,128)S(1)} %get-tuple-element.3) | data formatting | bytes 163840

commit v5 on v4

--- a/solution.py
+++ b/solution.py
@@ -45,7 +45,7 @@
 
     def for_right(table):
         high, low = halves(np.block([[table, zero], [zero, table]]))
-        return np.concatenate([high, high, low], 0)
+        return np.block([[high, low], [high, np.zeros_like(low)]])
 
     lefts = np.concatenate([for_left(basis), for_left(basis.T)], 0)
     rights = np.concatenate([for_right(basis.T), for_right(basis)], 0)
@@ -66,8 +66,8 @@
 
 def right(parts, table):
     high, low = halve(jnp.concatenate(parts, axis=0))
-    data = jnp.concatenate([high, low, high], axis=1)
-    tall = jnp.dot(data, table, preferred_element_type=jnp.float32)
+    tall = jnp.dot(jnp.concatenate([high, low], axis=1), table, preferred_element_type=jnp.float32)
+    tall = tall[:, :128] + tall[:, 128:]
     return [tall[SPAN * p : SPAN * p + SPAN] for p in range(3)]
 
 
@@ -80,7 +80,7 @@
     outm, outw,
     acts, outg, mom, wt, kept, lefts32, rights32, lefts, rights,
     part, rx, x1, x0, x2, zr, turned, names, tmsg, tin, every,
-    lsem, csend, crecv, xsend, xrecv, zsend, zrecv, nsend, nrecv, tsend, trecv, gsend, grecv,
+    lsem, csend, crecv, xsend, xrecv, zsend, zrecv, nsend, nrecv, tsend, trecv, gsend, grecv, told,
 ):
     rep = lax.axis_index("rep")
     f = lax.axis_index("fsdp")
@@ -116,7 +116,7 @@
 
     def greet_group(i, carry):
         pl.semaphore_signal(
-            barrier, inc=1, device_id=(rep, wrap(f + i, N_FSDP)), device_id_type=MESH
+            barrier, inc=1, device_id=(rep, wrap(f - core + 2 * i, N_FSDP)), device_id_type=MESH
         )
         return carry
 
@@ -126,8 +126,7 @@
         )
         return carry
 
-    lax.fori_loop(1, N_FSDP, greet_group, 0)
-    lax.fori_loop(1, N_REP, greet_peers, 0)
+    lax.fori_loop(1 - core, N_FSDP // 2, greet_group, 0)
 
     lane = lax.broadcasted_iota(jnp.int32, (32, 128), 1)
 
@@ -261,43 +260,48 @@
     def unpack(four):
         return jnp.concatenate([four, pltpu.roll(four, 104, 1)], axis=0)
 
-    def group_tiles(m, carry):
-        base = pl.multiple_of(m * WIDE, 128)
-        both = jnp.dot(turned[...], acts[:, pl.ds(base, WIDE)], preferred_element_type=jnp.float32)
-        both = both[0:128] + both[128:256]
+    def two_chunks(i, carry):
         numbers, rows = [], []
-        for h in range(2):
-            owner = ((2 * h + m // 4) * N_X + lax.rem(m, 4)) * 2
-            low = jnp.broadcast_to(names[owner], (TILE, 128))
-            high = jnp.broadcast_to(names[owner + 1], (TILE, 128))
-            ten = jnp.where(lane8 < 5, low, pltpu.roll(high, 5, 1))
-            for p in range(5):
-                number = jnp.take_along_axis(ten, jnp.where(lane8 < SPAN, 2 * p, 2 * p + 1), axis=1)
-                high_part = number >> 3
-                found = jnp.zeros((TILE, 128), jnp.float32)
-                for a in range(8):
-                    at_row = SPAN * h + TILE * a
-                    found = found + jnp.where(
-                        high_part == a, both[at_row : at_row + TILE, 128 * p : 128 * p + 128], 0.0
-                    )
-                numbers.append(number)
-                rows.append(found)
+        for c in range(2):
+            m = 2 * i + c
+            piece_acts = acts[:, pl.ds(pl.multiple_of(m * WIDE, 128), WIDE)]
+            both = jnp.dot(
+                turned[...], jnp.concatenate([piece_acts, piece_acts], axis=0),
+                preferred_element_type=jnp.float32,
+            )
+            for h in range(2):
+                owner = ((2 * h + m // 4) * N_X + lax.rem(m, 4)) * 2
+                low = jnp.broadcast_to(names[owner], (TILE, 128))
+                high = jnp.broadcast_to(names[owner + 1], (TILE, 128))
+                ten = jnp.where(lane8 < 5, low, pltpu.roll(high, 5, 1))
+                for p in range(5):
+                    number = jnp.take_along_axis(ten, 2 * p + jnp.where(lane8 < SPAN, 0, 1), axis=1)
+                    high_part = number >> 3
+                    found = both[SPAN * h : SPAN * h + TILE, 128 * p : 128 * p + 128]
+                    for a in range(1, 8):
+                        at_row = SPAN * h + TILE * a
+                        found = jnp.where(
+                            high_part == a, both[at_row : at_row + TILE, 128 * p : 128 * p + 128], found
+                        )
+                    numbers.append(number)
+                    rows.append(found)
         high, low = halve(jnp.concatenate(rows, axis=0))
-        data = jnp.concatenate([high, low, high], axis=1)
-        turned_rows = jnp.dot(data, rights[0:384], preferred_element_type=jnp.float32)
-        for h in range(2):
-            owner = ((2 * h + m // 4) * N_X + lax.rem(m, 4)) * 2
-            t = [
-                pick_columns(turned_rows[TILE * q : TILE * q + TILE], numbers[q])
-                for q in range(5 * h, 5 * h + 5)
-            ]
-            tmsg[owner] = pack(merge(t[0], t[1], t[2]))
-            tmsg[owner + 1] = pack(merge(t[3], t[4], pltpu.roll(t[2], SPAN, 1)))
+        out = jnp.dot(
+            jnp.concatenate([high, low], axis=1), rights[0:256], preferred_element_type=jnp.float32
+        )
+        out = out[:, :128] + out[:, 128:]
+        for c in range(2):
+            m = 2 * i + c
+            for h in range(2):
+                owner = ((2 * h + m // 4) * N_X + lax.rem(m, 4)) * 2
+                base = 10 * c + 5 * h
+                t = [
+                    pick_columns(out[TILE * q : TILE * q + TILE], numbers[q])
+                    for q in range(base, base + 5)
+                ]
+                tmsg[owner] = pack(merge(t[0], t[1], t[2]))
+                tmsg[owner + 1] = pack(merge(t[3], t[4], pltpu.roll(t[2], SPAN, 1)))
         return carry
-
-    def two_chunks(i, carry):
-        group_tiles(2 * i, carry)
-        return group_tiles(2 * i + 1, carry)
 
     def send_tiles():
         tin[f] = tmsg[f]
@@ -328,47 +332,43 @@
     load_outg.wait()
     flat = outg[...]
     grads = flat.astype(jnp.float32).T.astype(jnp.bfloat16)
+    for copy in small:
+        copy.wait()
+    lefts[...] = lefts32[...].astype(jnp.bfloat16)
+    rights[...] = rights32[...].astype(jnp.bfloat16)
+    fwd_l, inv_l = lefts[0:64, 0:192], lefts[64:128, 0:192]
+    fwd_r, inv_r = rights[0:256], rights[256:512]
+    spun = jnp.dot(flat, rights[0:128], preferred_element_type=jnp.float32)
+    spun_high, spun_low = halve((spun[:, :128] + spun[:, 128:]).T)
+    turned[:, :128] = spun_high
+    turned[:, 128:] = spun_low
     load_acts[0].wait()
-    pl.semaphore_wait(barrier, N_FSDP - 1 + N_REP - 1)
-    chunk(0, 0, grads)
-    chunk(0, 1, grads)
-    chunk(0, 2, grads)
+    sibling = (rep, f + 1 - 2 * core)
+
+    @pl.when(core == 0)
+    def _():
+        pl.semaphore_wait(barrier, N_FSDP - 1)
+        pl.semaphore_signal(told, inc=1, device_id=sibling, device_id_type=MESH)
+
+    @pl.when(core == 1)
+    def _():
+        pl.semaphore_wait(told, 1)
+        lax.fori_loop(1, N_REP, greet_peers, 0)
+
+    send_names()
+    for o in range(3):
+        chunk(0, o, grads)
     open_far(0)
     open_far(1)
     chunk(0, 3, grads)
     open_near(0)
     open_near(1)
-    for copy in small:
-        copy.wait()
-    send_names()
     load_acts[1].wait()
-    chunk(1, 0, grads)
-    pass_on(0)
-    chunk(1, 1, grads)
-    chunk(1, 2, grads)
-    open_far(2)
-    pass_on(1)
-    open_far(3)
-    chunk(1, 3, grads)
-    open_near(2)
-
-    lefts[...] = lefts32[...].astype(jnp.bfloat16)
-    rights[...] = rights32[...].astype(jnp.bfloat16)
-    fwd_l, inv_l = lefts[0:64, 0:192], lefts[64:128, 0:192]
-    fwd_r, inv_r = rights[0:384], rights[384:768]
-    spun = jnp.dot(flat, rights[0:128], preferred_element_type=jnp.float32)
-    spun = spun + jnp.dot(flat, rights[256:384], preferred_element_type=jnp.float32)
-    spun_high, spun_low = halve(spun.T)
-    turned[0:128] = spun_high
-    turned[128:256] = spun_low
-    open_near(3)
     all_names().wait_recv()
-    lax.fori_loop(0, 2, two_chunks, 0)
-    pass_on(2)
-    lax.fori_loop(2, 4, two_chunks, 0)
+    lax.fori_loop(0, 4, two_chunks, 0)
     send_tiles()
-    pass_on(3)
-    close_piece(0)
+    for o in range(4):
+        chunk(1, o, grads)
 
     scalars = [kept[0, s] for s in order]
     carried = [decay_rate * m for m in pairs(mom)]
@@ -383,6 +383,19 @@
         for p in range(3)
     ]
     from_momentum = merge(*found)
+    open_far(2)
+    open_far(3)
+    open_near(2)
+    open_near(3)
+
+    @pl.when(core == 1)
+    def _():
+        pl.semaphore_wait(barrier, N_REP - 1)
+        pl.semaphore_signal(told, inc=1, device_id=sibling, device_id_type=MESH)
+
+    @pl.when(core == 0)
+    def _():
+        pl.semaphore_wait(told, 1)
 
     all_tiles().wait_recv()
     tiles = from_momentum + unpack(jnp.sum(tin[...], axis=0))
@@ -402,6 +415,11 @@
         ref = every.at[pl.ds(0, N_REP - 1)]
         return to_peer(ref, ref, gsend, grecv, 1)
 
+    pass_on(0)
+    pass_on(1)
+    pass_on(2)
+    close_piece(0)
+    pass_on(3)
     close_piece(1)
     close_piece(2)
     src_tile = [upper + TILE * p + lax.rem(lane8, TILE) for p in range(3)]
@@ -416,9 +434,22 @@
     for p in range(3):
         carried[p] = carried[p] - decoded[p]
     weights = pairs(wt)
+    close_piece(3)
+    total = part[core, z, x]
+    tail = jnp.concatenate([total[128:160], pltpu.roll(total[128:160], 64, 1)], axis=0)
+    for p, grown in enumerate((total[0:64], total[64:128], tail)):
+        carried[p] = carried[p] + grown
     for k in range(4):
         for o in range(4):
             swap(k, o).wait_send()
+        for kind in range(3):
+            for way in range(2):
+                hop(k, kind, way).wait_send()
+    for k in range(3):
+        zhop(k).wait()
+    rest = zr[0] + zr[1] + zr[2]
+    tail = jnp.concatenate([rest[128:160], pltpu.roll(rest[128:160], 64, 1)], axis=0)
+    unpair(outm.at[0], [carried[0] + rest[0:64], carried[1] + rest[64:128], carried[2] + tail])
     all_names().wait_send()
     all_tiles().wait_send()
     all_posts().wait_send()
@@ -449,19 +480,6 @@
         spread = jnp.sqrt(jnp.where(low, mean_lo, mean_hi) + epsilon)
         fresh.append(weights[p] - step_size * update[p] / spread)
     unpair(outw, fresh)
-
-    close_piece(3)
-    for k in range(4):
-        for kind in range(3):
-            for way in range(2):
-                hop(k, kind, way).wait_send()
-        if k < 3:
-            zhop(k).wait_send()
-    for k in range(3):
-        zhop(k).wait_recv()
-    total = part[core, z, x] + (zr[0] + zr[1] + zr[2])
-    tail = jnp.concatenate([total[128:160], pltpu.roll(total[128:160], 64, 1)], axis=0)
-    unpair(outm.at[0], [carried[0] + total[0:64], carried[1] + total[64:128], carried[2] + tail])
 
 
 def shards(activations, out_grad, momentum, weight, kept_tile):
@@ -484,16 +502,16 @@
                 vm((5, SPAN, SPAN), f32),
                 pltpu.SMEM((1, 5), jnp.int32),
                 vm((128, 256), f32),
-                vm((768, 128), f32),
+                vm((512, 256), f32),
                 vm((128, 256), jnp.bfloat16),
-                vm((768, 128), jnp.bfloat16),
+                vm((512, 256), jnp.bfloat16),
                 vm((2, N_ZLO, N_X, SLAB, 128), f32),
                 vm((N_ZLO, N_X, SLAB, 128), f32),
                 vm((4, 2, HALF, 128), f32),
                 vm((4, 2, HALF, 128), f32),
                 vm((4, 2, HALF, 128), f32),
                 vm((3, SLAB, 128), f32),
-                vm((2 * TOK, TOK), jnp.bfloat16),
+                vm((TOK, 2 * TOK), jnp.bfloat16),
                 vm((N_FSDP, 1, 128), jnp.int32),
                 vm((N_FSDP, TILE // 2, 128), f32),
                 vm((N_FSDP, TILE // 2, 128), f32),
@@ -511,6 +529,7 @@
                 dma,
                 dma,
                 dma,
+                pltpu.SemaphoreType.REGULAR,
             ],
             compiler_params=pltpu.CompilerParams(
                 collective_id=0, has_side_effects=True, vmem_limit_bytes=48 * 1024 * 1024

time: 47.5 us -> 39.8 us (0.84)
  Pallas kernels: 45.4 us -> 37.7 us
    pallas_call x1, Pallas kernels: 45.4 us -> 37.7 us  [shards(): pl.pallas_call(kernel, out_shape=(pltpu.VMEM(momentum.shape, f32), pltpu....]
where the time goes in v5:
time: 39.8 us; the launch traced here: 39.6 us
  Pallas kernels  37.7 us (95%)
  local copies, waits for them, and re-layouts  1.33 us (3%)
  between operations  0.64 us (2%)
    pallas_call x1, Pallas kernels, shards(): pl.pallas_call(kernel, out_shape=(pltpu.VMEM(momentum.shape, f32), pltpu....  37.7 us
    unnamed x2, local copies, waits for them, and re-layouts  1.33 us

profile of v5, /device:TPU:1, one launch (start us, length us, event | category | flops | bytes accessed | tf_op | source)
XLA Modules:
  0.0 39.6 jit_solution(2610739852081610517)
XLA Ops:
  0.6 37.7 %demo_step.1 = (f32[1,5,64,64]{3,2,1,0:T(8,128)S(1)}, f32[5,64,64]{2,1,0:T(8,128)S(1)}) custom-call(bf16[128,5120]{1,0:T(8,128)(2,1)} %acts_h.1, bf16[128,128]{1,0:T(8,128)(2,1)} %outg_h.1, f32[1,5,64,64]{3,2,1,0:T(8,128)} %mom_h.1, f32[5,64,64]{2,1,0:T(8,128)} %wt_h.1, s32[1,5]{1,0:T(1,128)} %kept_h.1, f32[128,256]{1,0:T(8,128)} %constant.4.clone.lefts_h, ...), custom_call_target="tpu_custom_call" | custom-call | tf_op jit(solution)/shard_map/demo_step/pallas_call | solution.py:490
  38.3 0.7 %copy.11 = f32[1,5,64,64]{3,2,1,0:T(8,128)} copy(f32[1,5,64,64]{3,2,1,0:T(8,128)S(1)} %get-tuple-element.2) | data formatting | bytes 163840
  39.0 0.7 %copy.12 = f32[5,64,64]{2,1,0:T(8,128)} copy(f32[5,64,64]{2,1,0:T(8,128)S(1)} %get-tuple-element.3) | data formatting | bytes 163840

commit v6 on v5

--- a/solution.py
+++ b/solution.py
@@ -13,6 +13,7 @@
 N_ZLO = 4
 N_REP = 16
 N_FSDP = 32
+HUB = 1
 SLAB = 160
 HALF = SLAB // 2
 TOK = 128
@@ -115,9 +116,12 @@
     barrier = pltpu.get_barrier_semaphore()
 
     def greet_group(i, carry):
-        pl.semaphore_signal(
-            barrier, inc=1, device_id=(rep, wrap(f - core + 2 * i, N_FSDP)), device_id_type=MESH
-        )
+        member = wrap(f + i, N_FSDP)
+
+        @pl.when(member != HUB)
+        def _():
+            pl.semaphore_signal(barrier, inc=1, device_id=(rep, member), device_id_type=MESH)
+
         return carry
 
     def greet_peers(i, carry):
@@ -126,7 +130,7 @@
         )
         return carry
 
-    lax.fori_loop(1 - core, N_FSDP // 2, greet_group, 0)
+    lax.fori_loop(1, N_FSDP, greet_group, 0)
 
     lane = lax.broadcasted_iota(jnp.int32, (32, 128), 1)
 
@@ -329,11 +333,29 @@
             half = parts[j // 2][:, SPAN * (j % 2) : SPAN * (j % 2) + SPAN]
             ref[order[j]] = half
 
+    @pl.when(f != HUB)
+    def _():
+        pl.semaphore_wait(barrier, N_FSDP - 1)
+
+    @pl.when(f == HUB - 1)
+    def _():
+        pl.semaphore_signal(told, inc=1, device_id=(rep, HUB), device_id_type=MESH)
+
+    @pl.when(f == HUB)
+    def _():
+        pl.semaphore_wait(told, 1)
+        lax.fori_loop(1, N_REP, greet_peers, 0)
+
+    small[2].wait()
+    send_names()
     load_outg.wait()
     flat = outg[...]
     grads = flat.astype(jnp.float32).T.astype(jnp.bfloat16)
-    for copy in small:
-        copy.wait()
+    load_acts[0].wait()
+    for o in range(3):
+        chunk(0, o, grads)
+    for i in (0, 1, 3, 4):
+        small[i].wait()
     lefts[...] = lefts32[...].astype(jnp.bfloat16)
     rights[...] = rights32[...].astype(jnp.bfloat16)
     fwd_l, inv_l = lefts[0:64, 0:192], lefts[64:128, 0:192]
@@ -342,31 +364,28 @@
     spun_high, spun_low = halve((spun[:, :128] + spun[:, 128:]).T)
     turned[:, :128] = spun_high
     turned[:, 128:] = spun_low
-    load_acts[0].wait()
-    sibling = (rep, f + 1 - 2 * core)
-
-    @pl.when(core == 0)
-    def _():
-        pl.semaphore_wait(barrier, N_FSDP - 1)
-        pl.semaphore_signal(told, inc=1, device_id=sibling, device_id_type=MESH)
-
-    @pl.when(core == 1)
-    def _():
-        pl.semaphore_wait(told, 1)
-        lax.fori_loop(1, N_REP, greet_peers, 0)
-
-    send_names()
-    for o in range(3):
-        chunk(0, o, grads)
+    chunk(0, 3, grads)
     open_far(0)
     open_far(1)
-    chunk(0, 3, grads)
     open_near(0)
     open_near(1)
     load_acts[1].wait()
     all_names().wait_recv()
     lax.fori_loop(0, 4, two_chunks, 0)
     send_tiles()
+
+    def tell(i, carry):
+        member = wrap(f + i, N_FSDP)
+        pl.semaphore_signal(told, inc=1, device_id=(rep, member), device_id_type=MESH)
+        return carry
+
+    @pl.when(f == HUB)
+    def _():
+        pl.semaphore_wait(barrier, N_REP - 1)
+        lax.fori_loop(1, N_FSDP, tell, 0)
+
+    pass_on(0)
+    pass_on(1)
     for o in range(4):
         chunk(1, o, grads)
 
@@ -383,19 +402,6 @@
         for p in range(3)
     ]
     from_momentum = merge(*found)
-    open_far(2)
-    open_far(3)
-    open_near(2)
-    open_near(3)
-
-    @pl.when(core == 1)
-    def _():
-        pl.semaphore_wait(barrier, N_REP - 1)
-        pl.semaphore_signal(told, inc=1, device_id=sibling, device_id_type=MESH)
-
-    @pl.when(core == 0)
-    def _():
-        pl.semaphore_wait(told, 1)
 
     all_tiles().wait_recv()
     tiles = from_momentum + unpack(jnp.sum(tin[...], axis=0))
@@ -405,6 +411,10 @@
         message = jnp.where(spot, scalars[j].astype(jnp.float32), message)
     every[rep] = message
 
+    @pl.when(f != HUB)
+    def _():
+        pl.semaphore_wait(told, 1)
+
     def send_one(i, carry):
         to_peer(every.at[rep], every.at[rep], gsend, grecv, i).start()
         return carry
@@ -415,8 +425,10 @@
         ref = every.at[pl.ds(0, N_REP - 1)]
         return to_peer(ref, ref, gsend, grecv, 1)
 
-    pass_on(0)
-    pass_on(1)
+    open_far(2)
+    open_far(3)
+    open_near(2)
+    open_near(3)
     pass_on(2)
     close_piece(0)
     pass_on(3)

time: 39.8 us -> 41.9 us (1.053)
  Pallas kernels: 37.7 us -> 39.8 us
    pallas_call x1, Pallas kernels: 37.7 us -> 39.8 us  [shards(): pl.pallas_call(kernel, out_shape=(pltpu.VMEM(momentum.shape, f32), pltpu....]
where the time goes in v6:
time: 41.9 us; the launch traced here: 41.8 us
  Pallas kernels  39.8 us (95%)
  local copies, waits for them, and re-layouts  1.33 us (3%)
  between operations  0.64 us (2%)
    pallas_call x1, Pallas kernels, shards(): pl.pallas_call(kernel, out_shape=(pltpu.VMEM(momentum.shape, f32), pltpu....  39.8 us
    unnamed x2, local copies, waits for them, and re-layouts  1.33 us

profile of v6, /device:TPU:1, one launch (start us, length us, event | category | flops | bytes accessed | tf_op | source)
XLA Modules:
  0.0 41.8 jit_solution(3744898930246979477)
XLA Ops:
  0.6 39.8 %demo_step.1 = (f32[1,5,64,64]{3,2,1,0:T(8,128)S(1)}, f32[5,64,64]{2,1,0:T(8,128)S(1)}) custom-call(bf16[128,5120]{1,0:T(8,128)(2,1)} %acts_h.1, bf16[128,128]{1,0:T(8,128)(2,1)} %outg_h.1, f32[1,5,64,64]{3,2,1,0:T(8,128)} %mom_h.1, f32[5,64,64]{2,1,0:T(8,128)} %wt_h.1, s32[1,5]{1,0:T(1,128)} %kept_h.1, f32[128,256]{1,0:T(8,128)} %constant.4.clone.lefts_h, ...), custom_call_target="tpu_custom_call" | custom-call | tf_op jit(solution)/shard_map/demo_step/pallas_call | solution.py:502
  40.5 0.7 %copy.11 = f32[1,5,64,64]{3,2,1,0:T(8,128)} copy(f32[1,5,64,64]{3,2,1,0:T(8,128)S(1)} %get-tuple-element.2) | data formatting | bytes 163840
  41.1 0.7 %copy.12 = f32[5,64,64]{2,1,0:T(8,128)} copy(f32[5,64,64]{2,1,0:T(8,128)S(1)} %get-tuple-element.3) | data formatting | bytes 163840

commit v7 on v6

--- a/solution.py
+++ b/solution.py
@@ -379,15 +379,19 @@
         pl.semaphore_signal(told, inc=1, device_id=(rep, member), device_id_type=MESH)
         return carry
 
+    pass_on(0)
+    pass_on(1)
+    for o in range(4):
+        chunk(1, o, grads)
+    open_far(2)
+    open_far(3)
+    open_near(2)
+    open_near(3)
+
     @pl.when(f == HUB)
     def _():
         pl.semaphore_wait(barrier, N_REP - 1)
         lax.fori_loop(1, N_FSDP, tell, 0)
-
-    pass_on(0)
-    pass_on(1)
-    for o in range(4):
-        chunk(1, o, grads)
 
     scalars = [kept[0, s] for s in order]
     carried = [decay_rate * m for m in pairs(mom)]
@@ -425,10 +429,6 @@
         ref = every.at[pl.ds(0, N_REP - 1)]
         return to_peer(ref, ref, gsend, grecv, 1)
 
-    open_far(2)
-    open_far(3)
-    open_near(2)
-    open_near(3)
     pass_on(2)
     close_piece(0)
     pass_on(3)

time: 41.9 us -> 39.6 us (0.945)
  Pallas kernels: 39.8 us -> 37.5 us
    pallas_call x1, Pallas kernels: 39.8 us -> 37.5 us  [shards(): pl.pallas_call(kernel, out_shape=(pltpu.VMEM(momentum.shape, f32), pltpu....]
where the time goes in v7:
time: 39.6 us; the launch traced here: 39.4 us
  Pallas kernels  37.5 us (95%)
  local copies, waits for them, and re-layouts  1.33 us (3%)
  between operations  0.64 us (2%)
    pallas_call x1, Pallas kernels, shards(): pl.pallas_call(kernel, out_shape=(pltpu.VMEM(momentum.shape, f32), pltpu....  37.5 us
    unnamed x2, local copies, waits for them, and re-layouts  1.33 us

profile of v7, /device:TPU:1, one launch (start us, length us, event | category | flops | bytes accessed | tf_op | source)
XLA Modules:
  0.0 39.4 jit_solution(2861785512933658512)
XLA Ops:
  0.6 37.5 %demo_step.1 = (f32[1,5,64,64]{3,2,1,0:T(8,128)S(1)}, f32[5,64,64]{2,1,0:T(8,128)S(1)}) custom-call(bf16[128,5120]{1,0:T(8,128)(2,1)} %acts_h.1, bf16[128,128]{1,0:T(8,128)(2,1)} %outg_h.1, f32[1,5,64,64]{3,2,1,0:T(8,128)} %mom_h.1, f32[5,64,64]{2,1,0:T(8,128)} %wt_h.1, s32[1,5]{1,0:T(1,128)} %kept_h.1, f32[128,256]{1,0:T(8,128)} %constant.4.clone.lefts_h, ...), custom_call_target="tpu_custom_call" | custom-call | tf_op jit(solution)/shard_map/demo_step/pallas_call | solution.py:502
  38.1 0.7 %copy.11 = f32[1,5,64,64]{3,2,1,0:T(8,128)} copy(f32[1,5,64,64]{3,2,1,0:T(8,128)S(1)} %get-tuple-element.2) | data formatting | bytes 163840
  38.8 0.7 %copy.12 = f32[5,64,64]{2,1,0:T(8,128)} copy(f32[5,64,64]{2,1,0:T(8,128)S(1)} %get-tuple-element.3) | data formatting | bytes 163840

commit v8 on v7

--- a/solution.py
+++ b/solution.py
@@ -379,14 +379,19 @@
         pl.semaphore_signal(told, inc=1, device_id=(rep, member), device_id_type=MESH)
         return carry
 
-    pass_on(0)
-    pass_on(1)
-    for o in range(4):
-        chunk(1, o, grads)
-    open_far(2)
-    open_far(3)
-    open_near(2)
-    open_near(3)
+    def second_half():
+        pass_on(0)
+        pass_on(1)
+        chunk(1, 2, grads)
+        chunk(1, 3, grads)
+        open_far(2)
+        open_far(3)
+        open_near(2)
+        open_near(3)
+
+    chunk(1, 0, grads)
+    chunk(1, 1, grads)
+    pl.when(rep < N_REP // 4)(second_half)
 
     @pl.when(f == HUB)
     def _():
@@ -429,6 +434,7 @@
         ref = every.at[pl.ds(0, N_REP - 1)]
         return to_peer(ref, ref, gsend, grecv, 1)
 
+    pl.when(rep >= N_REP // 4)(second_half)
     pass_on(2)
     close_piece(0)
     pass_on(3)

time: 39.6 us -> 39.5 us (level)
  no operation moved by 1% of the time
where the time goes in v8:
time: 39.5 us; the launch traced here: 39.4 us
  Pallas kernels  37.4 us (95%)
  local copies, waits for them, and re-layouts  1.33 us (3%)
  between operations  0.64 us (2%)
    pallas_call x1, Pallas kernels, shards(): pl.pallas_call(kernel, out_shape=(pltpu.VMEM(momentum.shape, f32), pltpu....  37.4 us
    unnamed x2, local copies, waits for them, and re-layouts  1.33 us

profile of v8, /device:TPU:1, one launch (start us, length us, event | category | flops | bytes accessed | tf_op | source)
XLA Modules:
  0.0 39.4 jit_solution(3496019830617045000)
XLA Ops:
  0.6 37.4 %demo_step.1 = (f32[1,5,64,64]{3,2,1,0:T(8,128)S(1)}, f32[5,64,64]{2,1,0:T(8,128)S(1)}) custom-call(bf16[128,5120]{1,0:T(8,128)(2,1)} %acts_h.1, bf16[128,128]{1,0:T(8,128)(2,1)} %outg_h.1, f32[1,5,64,64]{3,2,1,0:T(8,128)} %mom_h.1, f32[5,64,64]{2,1,0:T(8,128)} %wt_h.1, s32[1,5]{1,0:T(1,128)} %kept_h.1, f32[128,256]{1,0:T(8,128)} %constant.4.clone.lefts_h, ...), custom_call_target="tpu_custom_call" | custom-call | tf_op jit(solution)/shard_map/demo_step/pallas_call | solution.py:508
  38.1 0.7 %copy.11 = f32[1,5,64,64]{3,2,1,0:T(8,128)} copy(f32[1,5,64,64]{3,2,1,0:T(8,128)S(1)} %get-tuple-element.2) | data formatting | bytes 163840
  38.7 0.7 %copy.12 = f32[5,64,64]{2,1,0:T(8,128)} copy(f32[5,64,64]{2,1,0:T(8,128)S(1)} %get-tuple-element.3) | data formatting | bytes 163840

commit v9 on v7

--- a/solution.py
+++ b/solution.py
@@ -370,23 +370,45 @@
     open_near(0)
     open_near(1)
     load_acts[1].wait()
+    early = rep < N_REP // 4
+
+    @pl.when(early)
+    def _():
+        for o in range(4):
+            chunk(1, o, grads)
+        open_far(2)
+        open_far(3)
+        open_near(2)
+        open_near(3)
+
     all_names().wait_recv()
-    lax.fori_loop(0, 4, two_chunks, 0)
+    lax.fori_loop(0, 2, two_chunks, 0)
+
+    @pl.when(early)
+    def _():
+        pass_on(0)
+        pass_on(1)
+
+    lax.fori_loop(2, 4, two_chunks, 0)
     send_tiles()
+
+    @pl.when(early)
+    def _():
+        pass_on(2)
+        close_piece(0)
+        pass_on(3)
+        close_piece(1)
+        close_piece(2)
+
+    @pl.when(jnp.logical_not(early))
+    def _():
+        chunk(1, 0, grads)
+        chunk(1, 1, grads)
 
     def tell(i, carry):
         member = wrap(f + i, N_FSDP)
         pl.semaphore_signal(told, inc=1, device_id=(rep, member), device_id_type=MESH)
         return carry
-
-    pass_on(0)
-    pass_on(1)
-    for o in range(4):
-        chunk(1, o, grads)
-    open_far(2)
-    open_far(3)
-    open_near(2)
-    open_near(3)
 
     @pl.when(f == HUB)
     def _():
@@ -429,11 +451,22 @@
         ref = every.at[pl.ds(0, N_REP - 1)]
         return to_peer(ref, ref, gsend, grecv, 1)
 
-    pass_on(2)
-    close_piece(0)
-    pass_on(3)
-    close_piece(1)
-    close_piece(2)
+    @pl.when(jnp.logical_not(early))
+    def _():
+        pass_on(0)
+        pass_on(1)
+        chunk(1, 2, grads)
+        chunk(1, 3, grads)
+        open_far(2)
+        open_far(3)
+        open_near(2)
+        open_near(3)
+        pass_on(2)
+        close_piece(0)
+        pass_on(3)
+        close_piece(1)
+        close_piece(2)
+
     src_tile = [upper + TILE * p + lax.rem(lane8, TILE) for p in range(3)]
     src_num = [56 + jnp.where(lane8 < SPAN, 2 * p, min(2 * p + 1, 4)) for p in range(3)]
 

time: 39.6 us -> 39.5 us (level)
  no operation moved by 1% of the time
where the time goes in v9:
time: 39.5 us; the launch traced here: 39.4 us
  Pallas kernels  37.4 us (95%)
  local copies, waits for them, and re-layouts  1.33 us (3%)
  between operations  0.64 us (2%)
    pallas_call x1, Pallas kernels, shards(): pl.pallas_call(kernel, out_shape=(pltpu.VMEM(momentum.shape, f32), pltpu....  37.4 us
    unnamed x2, local copies, waits for them, and re-layouts  1.33 us

profile of v9, /device:TPU:1, one launch (start us, length us, event | category | flops | bytes accessed | tf_op | source)
XLA Modules:
  0.0 39.4 jit_solution(13080680876324852518)
XLA Ops:
  0.6 37.4 %demo_step.1 = (f32[1,5,64,64]{3,2,1,0:T(8,128)S(1)}, f32[5,64,64]{2,1,0:T(8,128)S(1)}) custom-call(bf16[128,5120]{1,0:T(8,128)(2,1)} %acts_h.1, bf16[128,128]{1,0:T(8,128)(2,1)} %outg_h.1, f32[1,5,64,64]{3,2,1,0:T(8,128)} %mom_h.1, f32[5,64,64]{2,1,0:T(8,128)} %wt_h.1, s32[1,5]{1,0:T(1,128)} %kept_h.1, f32[128,256]{1,0:T(8,128)} %constant.4.clone.lefts_h, ...), custom_call_target="tpu_custom_call" | custom-call | tf_op jit(solution)/shard_map/demo_step/pallas_call | solution.py:535
  38.1 0.7 %copy.11 = f32[1,5,64,64]{3,2,1,0:T(8,128)} copy(f32[1,5,64,64]{3,2,1,0:T(8,128)S(1)} %get-tuple-element.2) | data formatting | bytes 163840
  38.7 0.7 %copy.12 = f32[5,64,64]{2,1,0:T(8,128)} copy(f32[5,64,64]{2,1,0:T(8,128)S(1)} %get-tuple-element.3) | data formatting | bytes 163840

commit v10 on v9

--- a/solution.py
+++ b/solution.py
@@ -365,15 +365,18 @@
     turned[:, :128] = spun_high
     turned[:, 128:] = spun_low
     chunk(0, 3, grads)
-    open_far(0)
-    open_far(1)
-    open_near(0)
-    open_near(1)
     load_acts[1].wait()
     early = rep < N_REP // 4
 
+    def first_half():
+        open_far(0)
+        open_far(1)
+        open_near(0)
+        open_near(1)
+
     @pl.when(early)
     def _():
+        first_half()
         for o in range(4):
             chunk(1, o, grads)
         open_far(2)
@@ -389,6 +392,7 @@
         pass_on(0)
         pass_on(1)
 
+    pl.when(jnp.logical_not(early))(first_half)
     lax.fori_loop(2, 4, two_chunks, 0)
     send_tiles()
 

time: 39.5 us -> 40.8 us (1.033)
  Pallas kernels: 37.4 us -> 38.7 us
    pallas_call x1, Pallas kernels: 37.4 us -> 38.7 us  [shards(): pl.pallas_call(kernel, out_shape=(pltpu.VMEM(momentum.shape, f32), pltpu....]
where the time goes in v10:
time: 40.8 us; the launch traced here: 40.7 us
  Pallas kernels  38.7 us (95%)
  local copies, waits for them, and re-layouts  1.33 us (3%)
  between operations  0.64 us (2%)
    pallas_call x1, Pallas kernels, shards(): pl.pallas_call(kernel, out_shape=(pltpu.VMEM(momentum.shape, f32), pltpu....  38.7 us
    unnamed x2, local copies, waits for them, and re-layouts  1.33 us

profile of v10, /device:TPU:1, one launch (start us, length us, event | category | flops | bytes accessed | tf_op | source)
XLA Modules:
  0.0 40.7 jit_solution(13603864599215528019)
XLA Ops:
  0.6 38.7 %demo_step.1 = (f32[1,5,64,64]{3,2,1,0:T(8,128)S(1)}, f32[5,64,64]{2,1,0:T(8,128)S(1)}) custom-call(bf16[128,5120]{1,0:T(8,128)(2,1)} %acts_h.1, bf16[128,128]{1,0:T(8,128)(2,1)} %outg_h.1, f32[1,5,64,64]{3,2,1,0:T(8,128)} %mom_h.1, f32[5,64,64]{2,1,0:T(8,128)} %wt_h.1, s32[1,5]{1,0:T(1,128)} %kept_h.1, f32[128,256]{1,0:T(8,128)} %constant.4.clone.lefts_h, ...), custom_call_target="tpu_custom_call" | custom-call | tf_op jit(solution)/shard_map/demo_step/pallas_call | solution.py:539
  39.4 0.7 %copy.11 = f32[1,5,64,64]{3,2,1,0:T(8,128)} copy(f32[1,5,64,64]{3,2,1,0:T(8,128)S(1)} %get-tuple-element.2) | data formatting | bytes 163840
  40.0 0.7 %copy.12 = f32[5,64,64]{2,1,0:T(8,128)} copy(f32[5,64,64]{2,1,0:T(8,128)S(1)} %get-tuple-element.3) | data formatting | bytes 163840

commit v11 on v9

--- a/solution.py
+++ b/solution.py
@@ -13,7 +13,7 @@
 N_ZLO = 4
 N_REP = 16
 N_FSDP = 32
-HUB = 1
+HUB = 31
 SLAB = 160
 HALF = SLAB // 2
 TOK = 128

time: 39.5 us -> 39.5 us (level)
  no operation moved by 1% of the time
where the time goes in v11:
time: 39.5 us; the launch traced here: 39.4 us
  Pallas kernels  37.4 us (95%)
  local copies, waits for them, and re-layouts  1.33 us (3%)
  between operations  0.64 us (2%)
    pallas_call x1, Pallas kernels, shards(): pl.pallas_call(kernel, out_shape=(pltpu.VMEM(momentum.shape, f32), pltpu....  37.4 us
    unnamed x2, local copies, waits for them, and re-layouts  1.33 us

profile of v11, /device:TPU:1, one launch (start us, length us, event | category | flops | bytes accessed | tf_op | source)
XLA Modules:
  0.0 39.4 jit_solution(7481719649274953258)
XLA Ops:
  0.6 37.4 %demo_step.1 = (f32[1,5,64,64]{3,2,1,0:T(8,128)S(1)}, f32[5,64,64]{2,1,0:T(8,128)S(1)}) custom-call(bf16[128,5120]{1,0:T(8,128)(2,1)} %acts_h.1, bf16[128,128]{1,0:T(8,128)(2,1)} %outg_h.1, f32[1,5,64,64]{3,2,1,0:T(8,128)} %mom_h.1, f32[5,64,64]{2,1,0:T(8,128)} %wt_h.1, s32[1,5]{1,0:T(1,128)} %kept_h.1, f32[128,256]{1,0:T(8,128)} %constant.4.clone.lefts_h, ...), custom_call_target="tpu_custom_call" | custom-call | tf_op jit(solution)/shard_map/demo_step/pallas_call | solution.py:535
  38.1 0.7 %copy.11 = f32[1,5,64,64]{3,2,1,0:T(8,128)} copy(f32[1,5,64,64]{3,2,1,0:T(8,128)S(1)} %get-tuple-element.2) | data formatting | bytes 163840
  38.7 0.7 %copy.12 = f32[5,64,64]{2,1,0:T(8,128)} copy(f32[5,64,64]{2,1,0:T(8,128)S(1)} %get-tuple-element.3) | data formatting | bytes 163840
